TPU v7x, 256 devices: a whole 4x4x8 slice. The times are simulated.
256 devices in a mesh: pb: 64 (over z, x, core), ka: 4 (over y).
Axes of the slice: x: 4, y: 4, z: 8, core: 2. Of those that a mesh axis runs over, the one named last changes fastest.
Arguments:
- queries: bfloat16 [65536, 512], P('pb'), may hold values from -80 to 80
- key_cache: bfloat16 [65536, 128], P(('ka', 'pb')), may hold values from -4.1 to 4.1
- value_cache: bfloat16 [65536, 128], P(('ka', 'pb')), may hold values from -4 to 4
- block_list: int32 [512, 32], P('pb'), may hold values from 0 to 511, as said below
- block_count: int32 [512], P('pb'), may hold values from 1 to 32, as said below
Outputs:
- attended: bfloat16 [65536, 512], P(('pb', 'ka'))
Inputs may be any that keep to these rules, and one draw needn't show every extreme that they name: `block_list`: entries of row qb before block_count[qb] are distinct blocks at most qb, and qb itself is among them. They are the blocks v at most qb of one set of 16 vertical blocks, then the blocks qb - o at least 0 (and not already listed) of one set of 16 slash offsets; both sets contain 0 and lie below 128. Later entries equal qb. `block_count`: the number of distinct listed blocks of each query block.
All inputs are finite; a program needn't handle non-finite values.
Results may differ from a plain program's by a relative error of at most 0.0046.
Values may be sent and summed in bfloat16 or wider, within the bound.
A program may use at most 128 MiB of HBM per device.

v0:
```python
import math

import jax
import jax.numpy as jnp
from jax import lax
from jax.sharding import PartitionSpec as P

HD = 128
QH = 4
BLK = 128
LIST = 32


masked_score = -1e30


def merged(shard, axis, combine):
    everything = jax.tree.map(lambda part: lax.all_gather(part, axis), shard)
    initial = jax.tree.map(lambda part: part[0], everything)

    def lap(k, so_far):
        return combine(so_far, jax.tree.map(lambda part: part[k], everything))

    return lax.fori_loop(1, lax.axis_size(axis), lap, initial)


def combine(first, second):
    peak_first, sum_first, out_first = first
    peak_second, sum_second, out_second = second
    peak_both = jnp.maximum(peak_first, peak_second)
    factor_first = jnp.exp(peak_first - peak_both)
    factor_second = jnp.exp(peak_second - peak_both)
    sum_both = factor_first * sum_first + factor_second * sum_second
    out_both = (
        jnp.repeat(factor_first, HD, axis=1) * out_first
        + jnp.repeat(factor_second, HD, axis=1) * out_second
    )
    return (peak_both, sum_both, out_both)


def shards(queries, key_cache, value_cache, block_list, block_count):
    shard_keys, shard_values = (
        lax.all_gather(key_cache, "pb", axis=0, tiled=True),
        lax.all_gather(value_cache, "pb", axis=0, tiled=True),
    )
    group_index = lax.axis_index("pb")
    shard_index = lax.axis_index("ka")
    ka_width = lax.axis_size("ka")
    score_scale = 1.0 / math.sqrt(HD)
    shard_width = shard_keys.shape[0] // BLK
    local_blocks = queries.shape[0] // BLK
    first_block = shard_index * shard_width
    all_key_tiles = shard_keys.reshape(shard_width, BLK, HD)
    all_value_tiles = shard_values.reshape(shard_width, BLK, HD)
    slot_ids = jnp.arange(LIST, dtype=jnp.int32)
    position = jnp.arange(BLK, dtype=jnp.int32)

    def one_block(block_pos):
        query_rows = lax.dynamic_slice_in_dim(queries, block_pos * BLK, BLK, 0).reshape(BLK, QH, HD)
        listed = lax.dynamic_index_in_dim(block_list, block_pos, 0, keepdims=False)
        live_count = lax.dynamic_index_in_dim(block_count, block_pos, 0, keepdims=False)
        global_pos = group_index * local_blocks + block_pos
        live_slot = slot_ids < live_count
        local_ids = listed - first_block
        tile_live = live_slot & (local_ids >= 0) & (local_ids < shard_width)
        picked = jnp.clip(local_ids, 0, shard_width - 1)
        key_tiles = all_key_tiles[picked]
        value_tiles = all_value_tiles[picked]
        scores = (
            jnp.einsum("qhd,skd->hqsk", query_rows, key_tiles, preferred_element_type=jnp.float32)
            * score_scale
        )
        earlier = (listed < global_pos)[None, :, None]
        diagonal = (listed == global_pos)[None, :, None] & (
            position[None, None, :] <= position[:, None, None]
        )
        valid = tile_live[None, :, None] & (earlier | diagonal)
        masked = jnp.where(valid[None], scores, masked_score)
        peak_row = jnp.max(masked, axis=(2, 3))
        weights = jnp.where(valid[None], jnp.exp(scores - peak_row[..., None, None]), 0.0)
        weight_sum = jnp.sum(weights, axis=(2, 3))
        partial_out = jnp.einsum(
            "hqsk,skd->qhd",
            weights.astype(jnp.bfloat16),
            value_tiles,
            preferred_element_type=jnp.float32,
        )
        return (peak_row.T, weight_sum.T, partial_out.reshape(BLK, QH * HD))

    peaks, sums, outputs = lax.map(one_block, jnp.arange(local_blocks, dtype=jnp.int32))
    peaks = peaks.reshape(local_blocks * BLK, QH)
    sums = sums.reshape(local_blocks * BLK, QH)
    outputs = outputs.reshape(local_blocks * BLK, QH * HD)
    merged_peak, merged_sum, merged_out = merged((peaks, sums, outputs), "ka", combine)
    owned = merged_out.shape[0] // ka_width
    out_share = lax.dynamic_slice_in_dim(merged_out, shard_index * owned, owned, 0)
    sum_share = lax.dynamic_slice_in_dim(merged_sum, shard_index * owned, owned, 0)
    return (out_share / jnp.repeat(sum_share, HD, axis=1)).astype(jnp.bfloat16)


def solution(mesh):
    placed = (P("pb", None), P(("ka", "pb"), None), P(("ka", "pb"), None), P("pb", None), P("pb"))
    return jax.shard_map(
        shards, mesh=mesh, in_specs=placed, out_specs=P(("pb", "ka"), None), check_vma=False
    )
```

profile of v0, /device:TPU:95, one launch (start us, length us, event | category | flops | bytes accessed | tf_op | source)
XLA Modules:
  0.0 489.1 jit_solution(4541151159910000270)
XLA Ops:
  8.1 81.1 %all-gather.4.cloned.1.call-done = bf16[16384,128]{1,0:T(8,128)(2,1)} async-done(((bf16[256,128]{1,0:T(8,128)(2,1)}), bf16[16384,128]{1,0:T(8,128)(2,1)}) %all-gather.4.cloned.1.call-update) | async-done | bytes 4194320 | tf_op jit(solution)/shard_map/all_gather | solution.py:43
  89.2 79.1 %all-gather.6.cloned.1.call-done = bf16[16384,128]{1,0:T(8,128)(2,1)} async-done(((bf16[256,128]{1,0:T(8,128)(2,1)}), bf16[16384,128]{1,0:T(8,128)(2,1)}) %all-gather.6.cloned.1.call-update) | async-done | bytes 4194320 | tf_op jit(solution)/shard_map/all_gather | solution.py:44
  168.3 201.8 %while.37 = (s32[]{:T(128)}, f32[8,128,4]{1,2,0:T(4,128)S(1)}, f32[8,128,4]{1,2,0:T(4,128)S(1)}, f32[8,128,512]{2,1,0:T(8,128)}, s32[8]{0:T(128)S(1)}, /*index=5...) while((s32[]{:T(128)}, f32[8,128,4]{1,2,0:T(4,128)S(1)}, ...), condition=%wide.region_3.4_spmd.clone, body=%wide.region_0.3_spmd.clone.sunk | while | flops 1098400256 | bytes 69129872 | solution.py:90
  172.1 1.3 dynamic_slice.85
  177.1 2.9 gather_fusion
  181.3 1.9 fusion.40
  183.1 1.3 copy-done
  184.5 2.9 gather_fusion.1
  187.4 5.2 %fusion.41 = f32[128,4,128,1]{2,0,1,3:T(8,128)S(1)} fusion(f32[32,128,128,4]{2,1,3,0:T(8,128)} %copy-done, f32[4,128]{1,0:T(4,128)S(1)} %get-tuple-element.581, pred[128,32,128]{0,2,1:T(8,128)(4,1)S(1)} %or_and_fusion.2, bf16[32,128,128]{2,1,0:T(8,128)(2,1)S(1)} %gather_fusion.1), kind=kOutput, calls=%fused_computation.20.clone.1 | convolution fusion | flops 545259520 | bytes 10225664 | tf_op jit(solution)/shard_map/while/body/eval_jaxpr/hqsk,skd->qhd/dot_general | solution.py:82
  197.4 1.3 dynamic_slice.85
  202.3 2.9 gather_fusion
  206.5 1.9 fusion.40
  208.4 1.3 copy-done
  209.7 2.9 gather_fusion.1
  212.7 5.2 %fusion.41 = f32[128,4,128,1]{2,0,1,3:T(8,128)S(1)} fusion(f32[32,128,128,4]{2,1,3,0:T(8,128)} %copy-done, f32[4,128]{1,0:T(4,128)S(1)} %get-tuple-element.581, pred[128,32,128]{0,2,1:T(8,128)(4,1)S(1)} %or_and_fusion.2, bf16[32,128,128]{2,1,0:T(8,128)(2,1)S(1)} %gather_fusion.1), kind=kOutput, calls=%fused_computation.20.clone.1 | convolution fusion | flops 545259520 | bytes 10225664 | tf_op jit(solution)/shard_map/while/body/eval_jaxpr/hqsk,skd->qhd/dot_general | solution.py:82
  222.6 1.3 dynamic_slice.85
  224.5 1.3 or_and_fusion.2
  227.5 2.9 gather_fusion
  231.7 1.9 fusion.40
  233.6 1.3 copy-done
  234.9 2.9 gather_fusion.1
  237.9 5.2 %fusion.41 = f32[128,4,128,1]{2,0,1,3:T(8,128)S(1)} fusion(f32[32,128,128,4]{2,1,3,0:T(8,128)} %copy-done, f32[4,128]{1,0:T(4,128)S(1)} %get-tuple-element.581, pred[128,32,128]{0,2,1:T(8,128)(4,1)S(1)} %or_and_fusion.2, bf16[32,128,128]{2,1,0:T(8,128)(2,1)S(1)} %gather_fusion.1), kind=kOutput, calls=%fused_computation.20.clone.1 | convolution fusion | flops 545259520 | bytes 10225664 | tf_op jit(solution)/shard_map/while/body/eval_jaxpr/hqsk,skd->qhd/dot_general | solution.py:82
  247.8 1.3 dynamic_slice.85
  252.7 2.9 gather_fusion
  256.9 1.9 fusion.40
  258.8 1.3 copy-done
  260.2 2.9 gather_fusion.1
  263.1 5.2 %fusion.41 = f32[128,4,128,1]{2,0,1,3:T(8,128)S(1)} fusion(f32[32,128,128,4]{2,1,3,0:T(8,128)} %copy-done, f32[4,128]{1,0:T(4,128)S(1)} %get-tuple-element.581, pred[128,32,128]{0,2,1:T(8,128)(4,1)S(1)} %or_and_fusion.2, bf16[32,128,128]{2,1,0:T(8,128)(2,1)S(1)} %gather_fusion.1), kind=kOutput, calls=%fused_computation.20.clone.1 | convolution fusion | flops 545259520 | bytes 10225664 | tf_op jit(solution)/shard_map/while/body/eval_jaxpr/hqsk,skd->qhd/dot_general | solution.py:82
  273.0 1.3 dynamic_slice.85
  275.0 1.3 or_and_fusion.2
  277.9 2.9 gather_fusion
  282.1 1.9 fusion.40
  284.0 1.3 copy-done
  285.4 2.9 gather_fusion.1
  288.3 5.2 %fusion.41 = f32[128,4,128,1]{2,0,1,3:T(8,128)S(1)} fusion(f32[32,128,128,4]{2,1,3,0:T(8,128)} %copy-done, f32[4,128]{1,0:T(4,128)S(1)} %get-tuple-element.581, pred[128,32,128]{0,2,1:T(8,128)(4,1)S(1)} %or_and_fusion.2, bf16[32,128,128]{2,1,0:T(8,128)(2,1)S(1)} %gather_fusion.1), kind=kOutput, calls=%fused_computation.20.clone.1 | convolution fusion | flops 545259520 | bytes 10225664 | tf_op jit(solution)/shard_map/while/body/eval_jaxpr/hqsk,skd->qhd/dot_general | solution.py:82
  298.2 1.3 dynamic_slice.85
  303.2 2.9 gather_fusion
  307.4 1.9 fusion.40
  309.2 1.3 copy-done
  310.6 2.9 gather_fusion.1
  313.5 5.2 %fusion.41 = f32[128,4,128,1]{2,0,1,3:T(8,128)S(1)} fusion(f32[32,128,128,4]{2,1,3,0:T(8,128)} %copy-done, f32[4,128]{1,0:T(4,128)S(1)} %get-tuple-element.581, pred[128,32,128]{0,2,1:T(8,128)(4,1)S(1)} %or_and_fusion.2, bf16[32,128,128]{2,1,0:T(8,128)(2,1)S(1)} %gather_fusion.1), kind=kOutput, calls=%fused_computation.20.clone.1 | convolution fusion | flops 545259520 | bytes 10225664 | tf_op jit(solution)/shard_map/while/body/eval_jaxpr/hqsk,skd->qhd/dot_general | solution.py:82
  323.5 1.3 dynamic_slice.85
  325.4 1.3 or_and_fusion.2
  328.4 2.9 gather_fusion
  332.6 1.9 fusion.40
  334.5 1.3 copy-done
  335.8 2.9 gather_fusion.1
  338.8 5.2 %fusion.41 = f32[128,4,128,1]{2,0,1,3:T(8,128)S(1)} fusion(f32[32,128,128,4]{2,1,3,0:T(8,128)} %copy-done, f32[4,128]{1,0:T(4,128)S(1)} %get-tuple-element.581, pred[128,32,128]{0,2,1:T(8,128)(4,1)S(1)} %or_and_fusion.2, bf16[32,128,128]{2,1,0:T(8,128)(2,1)S(1)} %gather_fusion.1), kind=kOutput, calls=%fused_computation.20.clone.1 | convolution fusion | flops 545259520 | bytes 10225664 | tf_op jit(solution)/shard_map/while/body/eval_jaxpr/hqsk,skd->qhd/dot_general | solution.py:82
  348.7 1.3 dynamic_slice.85
  350.6 1.3 or_and_fusion.2
  353.6 2.9 gather_fusion
  357.8 1.9 fusion.40
  359.7 1.3 copy-done
  361.0 2.9 gather_fusion.1
  364.0 5.2 %fusion.41 = f32[128,4,128,1]{2,0,1,3:T(8,128)S(1)} fusion(f32[32,128,128,4]{2,1,3,0:T(8,128)} %copy-done, f32[4,128]{1,0:T(4,128)S(1)} %get-tuple-element.581, pred[128,32,128]{0,2,1:T(8,128)(4,1)S(1)} %or_and_fusion.2, bf16[32,128,128]{2,1,0:T(8,128)(2,1)S(1)} %gather_fusion.1), kind=kOutput, calls=%fused_computation.20.clone.1 | convolution fusion | flops 545259520 | bytes 10225664 | tf_op jit(solution)/shard_map/while/body/eval_jaxpr/hqsk,skd->qhd/dot_general | solution.py:82
  370.1 9.0 %all_gather.17 = f32[4,1024,4]{1,2,0:T(4,128)S(1)} all-gather(f32[1,1024,4]{1,2,0:T(4,128)S(1)} %bitcast.155), channel_id=1, replica_groups=mesh['pb'=64,'ka'=4] {'ka'}, dimensions={0}, use_global_device_ids=true | all-gather | bytes 81920 | tf_op jit(solution)/shard_map/all_gather | solution.py:18
  379.0 9.4 %all_gather.18 = f32[4,1024,4]{1,2,0:T(4,128)S(1)} all-gather(f32[1,1024,4]{1,2,0:T(4,128)S(1)} %bitcast.156), channel_id=1, replica_groups=mesh['pb'=64,'ka'=4] {'ka'}, dimensions={0}, use_global_device_ids=true | all-gather | bytes 81920 | tf_op jit(solution)/shard_map/all_gather | solution.py:18
  388.5 65.9 %all-gather.8.cloned.1.call-done = f32[4,1024,512]{2,1,0:T(8,128)} async-done(((f32[1,1024,512]{2,1,0:T(8,128)}), f32[4,1024,512]{2,1,0:T(8,128)}) %all-gather.8.cloned.1.call-update) | async-done | bytes 8388624 | tf_op jit(solution)/shard_map/all_gather | solution.py:18
  454.4 3.1 slice_bitcast_fusion
  457.5 22.8 %while.36 = (s32[]{:T(128)}, f32[1024,4]{0,1:T(4,128)S(1)}, f32[1024,4]{0,1:T(4,128)S(1)}, f32[1024,512]{1,0:T(8,128)}, f32[4,1024,4]{1,2,0:T(4,128)S(1)}, /*ind...) while((s32[]{:T(128)}, f32[1024,4]{0,1:T(4,128)S(1)}, ...), condition=%wide.region_5.6_spmd, body=%wide.region_4.5_spmd.sunk | while | flops 1597445 | bytes 14909591 | solution.py:24
  460.5 4.6 fusion.34
  468.0 4.6 fusion.34
  475.6 4.6 fusion.34
  480.7 1.8 fusion.21
  (146 shorter events, 56.7 us)
Async XLA Ops:
  6.5 82.7 %all-gather.4.cloned.1.call-start = ((), (), s32[]{:S(2)}) async-start(), calls=%async_computation | async-start | bytes 4259840 | tf_op jit(solution)/shard_map/all_gather | solution.py:43
  7.3 161.0 %all-gather.6.cloned.1.call-start = ((), (), s32[]{:S(2)}) async-start(), calls=%async_computation.1 | async-start | bytes 4259840 | tf_op jit(solution)/shard_map/all_gather | solution.py:44
  8.0 446.4 %all-gather.8.cloned.1.call-start = ((), (), s32[]{:S(2)}) async-start(), calls=%async_computation.2 | async-start | bytes 10485760 | tf_op jit(solution)/shard_map/all_gather | solution.py:18
  181.3 3.2 copy-start
  206.5 3.2 copy-start
  231.7 3.2 copy-start
  256.9 3.2 copy-start
  282.1 3.2 copy-start
  307.4 3.2 copy-start
  332.6 3.2 copy-start
  357.8 3.2 copy-start
Sparse Core Ops, SparseCore 0:
  10.1 79.0 all-gather.3
  92.0 76.2 all-gather.5
  370.2 84.1 all-gather.7
where the time goes:
time: 494 us; the launch traced here: 489 us
  waiting for transfers between devices  228 us (46%)
  local copies, waits for them, and re-layouts  101 us (20%)
  other arithmetic  51.8 us (10%)
  matrix products  51.4 us (10%)
  loops' own time  26.3 us (5%)
  blocking collectives  18.4 us (4%)
  between operations  13.2 us (3%)
    all_gather x1, waiting for transfers between devices, shards(): lax.all_gather(key_cache, 'pb', axis=0, tiled=True)  81.1 us
    all_gather x1, waiting for transfers between devices, shards(): lax.all_gather(value_cache, 'pb', axis=0, tiled=True)  79.1 us
    all_gather x1, waiting for transfers between devices, merged(): everything = jax.tree.map(lambda part: lax.all_gather(part, axis), shard)  65.9 us
    dot_general x8, matrix products, one_block(): jnp.einsum('hqsk,skd->qhd', weights.astype(jnp.bfloat16), value_tiles, pr...  41.5 us
    another operation x1, loops' own time, shards(): lax.map(one_block, jnp.arange(local_blocks, dtype=jnp.int32))  26.2 us
    gather x8, local copies, waits for them, and re-layouts, one_block(): key_tiles = all_key_tiles[picked]  23.5 us
    gather x8, local copies, waits for them, and re-layouts, one_block(): value_tiles = all_value_tiles[picked]  23.5 us
    all_gather x2, blocking collectives, merged(): everything = jax.tree.map(lambda part: lax.all_gather(part, axis), shard)  18.4 us
  transfers between devices with their start and end apart: 3, of which 3 were waited for; matrix products, arithmetic and copies ran while one was open for 0% of the time, Pallas kernels for 0%

commit v1 on v0

v1 whole, which is shorter than its diff:
```python
import functools
import math

import jax
import jax.numpy as jnp
from jax import lax
from jax.experimental import pallas as pl
from jax.experimental.pallas import tpu as pltpu
from jax.sharding import PartitionSpec as P

HD = 128
QH = 4
BLK = 128
LIST = 32
NV = 16
PART = 16
CHUNK = 4
MASKED = -1e30
FACTOR = math.log2(math.e) / math.sqrt(HD)


def attention_kernel(
    list_ref, count_ref, q_hbm, k_hbm, v_hbm, out_ref,
    buf, vbuf, qs, kc, vc, s_ref, acc_ref, m_ref, l_ref,
    q_sem, z_send, z_recv, p1_send, p1_recv, p2_send, p2_recv, sib_send, sib_recv,
    vz_send, vz_recv, vx_send, vx_recv, vy_send, vy_recv, vs_send, vs_recv,
):
    p = lax.axis_index("pb")
    y = lax.axis_index("ka")
    z = p // 8
    x = (p // 2) % 4
    c = p % 2

    def dev(zz, xx, cc, yy):
        return (zz * 8 + xx * 2 + cc, yy)

    def remote(src, dst, ssem, rsem, device):
        return pltpu.make_async_remote_copy(
            src_ref=src, dst_ref=dst, send_sem=ssem, recv_sem=rsem,
            device_id=device, device_id_type=pl.DeviceIdType.MESH,
        )

    def have(hi):
        return z >= 2 - hi

    def needed(hi, g, xx):
        if hi == 1:
            return have(hi)
        if hi == 0:
            return have(hi) & ((g >= xx) | (z == 2))
        return g <= xx

    q_copy = pltpu.make_async_copy(q_hbm.at[pl.ds(pl.multiple_of(y * 256, 256), 256)], qs, q_sem)
    q_copy.start()

    src = (k_hbm, v_hbm)
    g_own = z % 4

    def z_target(kv):
        return (x, g_own) if kv == 0 else (g_own, x)

    def z_plane(d):
        return 2 * y + z // 4 + d

    def z_copy(kv, d):
        xd, yd = z_target(kv)
        region = buf.at[kv, 2 - d, g_own, x, c]
        return remote(src[kv], region, z_send.at[kv, d], z_recv.at[kv, 2 - d], dev(z_plane(d), xd, c, yd))

    def z_self(kv, d):
        xd, yd = z_target(kv)
        return (z_plane(d) == z) & (xd == x) & (yd == y)

    for d in range(3):
        for kv in range(2):
            live = z_plane(d) <= 7
            own = z_self(kv, d)

            @pl.when(live & jnp.logical_not(own))
            def _():
                z_copy(kv, d).start()

            @pl.when(live & own)
            def _():
                pltpu.make_async_copy(src[kv], buf.at[kv, 2 - d, g_own, x, c], z_recv.at[kv, 2 - d]).start()

    def row(kv):
        return y if kv == 0 else x

    def col(kv):
        return x if kv == 0 else y

    def along(kv, i):
        return dev(z, (x + i) % 4, c, y) if kv == 0 else dev(z, x, c, (y + i) % 4)

    def across(kv, i):
        return dev(z, x, c, (y + i) % 4) if kv == 0 else dev(z, (x + i) % 4, c, y)

    sibling = dev(z, x, 1 - c, y)

    def p1_copy(kv, hi, i):
        region = buf.at[kv, hi, row(kv), col(kv), c]
        return remote(region, region, p1_send.at[kv, hi, i - 1], p1_recv.at[kv, hi, i - 1], along(kv, i))

    def p1_live(kv, hi, i):
        return needed(hi, y, (x + i) % 4) if kv == 0 else have(hi)

    def p2_copy(kv, hi, i):
        region = buf.at[kv, hi, row(kv), :, c]
        return remote(region, region, p2_send.at[kv, hi, i - 1], p2_recv.at[kv, hi, i - 1], across(kv, i))

    def p2_live(kv, hi, i):
        return needed(hi, y, x) if kv == 0 else needed(hi, x, (x + i) % 4)

    def sib_copy(kv, hi, g):
        region = buf.at[kv, hi, g, :, c]
        return remote(region, region, sib_send.at[kv, hi, g], sib_recv.at[kv, hi, g], sibling)

    for hi in (1, 2, 0):
        for kv in range(2):

            @pl.when(have(hi))
            def _():
                pltpu.make_async_copy(src[kv], buf.at[kv, hi, row(kv), col(kv), c], z_recv.at[kv, hi]).wait()

            for i in (1, 3, 2):

                @pl.when(p1_live(kv, hi, i))
                def _():
                    p1_copy(kv, hi, i).start()

    for hi in (1, 2, 0):
        for kv in range(2):
            for i in (1, 3, 2):
                got = needed(hi, y, x) if kv == 0 else have(hi)

                @pl.when(got)
                def _():
                    region = buf.at[kv, hi, row(kv), (col(kv) + 4 - i) % 4, c]
                    remote(region, region, p1_send.at[kv, hi, i - 1], p1_recv.at[kv, hi, i - 1], sibling).wait_recv()

            for i in (1, 3, 2):

                @pl.when(p2_live(kv, hi, i))
                def _():
                    p2_copy(kv, hi, i).start()

            @pl.when(needed(hi, row(kv), x))
            def _():
                sib_copy(kv, hi, row(kv)).start()

    for hi in (1, 2, 0):
        for i in (1, 3, 2):
            for kv in range(2):
                g = (row(kv) + 4 - i) % 4

                @pl.when(needed(hi, g, x))
                def _():
                    region = buf.at[kv, hi, g, :, c]
                    remote(region, region, p2_send.at[kv, hi, i - 1], p2_recv.at[kv, hi, i - 1], sibling).wait_recv()
                    sib_copy(kv, hi, g).start()

    for hi in (1, 2, 0):
        for kv in range(2):
            for g in range(4):

                @pl.when(needed(hi, g, x))
                def _():
                    region = buf.at[kv, hi, g, :, 1 - c]
                    remote(region, region, sib_send.at[kv, hi, g], sib_recv.at[kv, hi, g], sibling).wait_recv()

    def vz_copy(i):
        return remote(vbuf.at[c, x, y], vbuf.at[c, x, y], vz_send.at[i], vz_recv, dev(3 + i, x, c, y))

    def vx_copy(i):
        return remote(
            vbuf.at[c, x, y], vbuf.at[c, x, y], vx_send.at[i - 1], vx_recv.at[i - 1], dev(z, (x + i) % 4, c, y)
        )

    def vy_copy(i):
        return remote(
            vbuf.at[c, :, y], vbuf.at[c, :, y], vy_send.at[i - 1], vy_recv.at[i - 1], dev(z, x, c, (y + i) % 4)
        )

    def vs_copy(cc):
        return remote(vbuf.at[cc], vbuf.at[cc], vs_send, vs_recv, sibling)

    def place(block):
        rel = jnp.clip(block - 64 * (z - 2), 0, 191)
        return rel >> 6, (rel >> 4) & 3, (rel >> 2) & 3, (rel >> 1) & 1, rel & 1

    def block_of(kv, block):
        hi, g, l, cc, r = place(block)
        return buf[kv, hi, g, l, cc, r]

    @pl.when(z == 2)
    def _():
        entries = [list_ref[2 * y, i] for i in range(NV)]
        chosen = jnp.int32(0)
        for i in range(NV):
            rank = jnp.int32(0)
            for j in range(NV):
                if j != i:
                    rank = rank + jnp.where(entries[j] < entries[i], 1, 0)
            chosen = chosen + jnp.where(rank == 4 * x + y, entries[i], 0)
        vbuf[c, x, y] = block_of(c, chosen)
        for i in (0, 4, 1, 3, 2):
            vz_copy(i).start()

    @pl.when(z >= 3)
    def _():
        vz_copy(0).wait_recv()
        for i in (1, 3, 2):
            vx_copy(i).start()

    delta = lax.broadcasted_iota(jnp.int32, (BLK, BLK), 1) - lax.broadcasted_iota(jnp.int32, (BLK, BLK), 0)

    def load_part(part):
        def load(n, _):
            q = n // PART
            s = n % PART
            block = list_ref[2 * y + q, part * PART + s]
            rows = pl.ds(pl.multiple_of(s * BLK, BLK), BLK)
            kc[q, rows, :] = block_of(0, block)
            vc[q, rows, :] = block_of(1, block)
            return 0

        lax.fori_loop(0, 2 * PART, load, 0)

    def attend(q, part):
        my_block = 8 * p + 2 * y + q
        count = count_ref[2 * y + q]
        rows = pl.ds(pl.multiple_of(q * BLK, BLK), BLK)
        q4 = jnp.concatenate([qs[rows, h * HD : (h + 1) * HD] for h in range(QH)], axis=0)
        width = CHUNK * BLK
        peak = None
        for n in range(PART // CHUNK):
            keys = kc[q, n * width : (n + 1) * width, :]
            scores = lax.dot_general(q4, keys, (((1,), (1,)), ((), ())), preferred_element_type=jnp.float32)
            for k in range(CHUNK):
                slot = part * PART + n * CHUNK + k
                block = list_ref[2 * y + q, slot]
                reach = jnp.where(block == my_block, 0, BLK)
                reach = jnp.where(slot < count, reach, -BLK)
                ok = delta <= reach
                tile = scores[:, k * BLK : (k + 1) * BLK].reshape(QH, BLK, BLK)
                tile = jnp.where(ok[None], tile, MASKED).reshape(QH * BLK, BLK)
                s_ref[:, (n * CHUNK + k) * BLK : (n * CHUNK + k + 1) * BLK] = tile
                peak = tile if peak is None else jnp.maximum(peak, tile)
        top = jnp.max(peak, axis=1, keepdims=True)
        total = None
        acc = None
        for n in range(PART // CHUNK):
            weights = jnp.exp2((s_ref[:, n * width : (n + 1) * width] - top) * FACTOR)
            for k in range(CHUNK):
                tile = weights[:, k * BLK : (k + 1) * BLK]
                total = tile if total is None else total + tile
            values = vc[q, n * width : (n + 1) * width, :]
            out = jnp.dot(weights.astype(jnp.bfloat16), values, preferred_element_type=jnp.float32)
            acc = out if acc is None else acc + out
        return top, jnp.sum(total, axis=1, keepdims=True), acc

    load_part(1)
    q_copy.wait()

    def first(q, _):
        top, total, acc = attend(q, 1)
        acc_ref[q] = acc
        m_ref[q] = jnp.broadcast_to(top, (QH * BLK, HD))
        l_ref[q] = jnp.broadcast_to(total, (QH * BLK, HD))
        return 0

    lax.fori_loop(0, 1, first, 0)

    @pl.when(z >= 3)
    def _():
        for i in (1, 3, 2):
            region = vbuf.at[c, (x + 4 - i) % 4, y]
            remote(region, region, vx_send.at[i - 1], vx_recv.at[i - 1], sibling).wait_recv()
        for i in (1, 3, 2):
            vy_copy(i).start()

    lax.fori_loop(1, 2, first, 0)

    @pl.when(z >= 3)
    def _():
        for i in (1, 3, 2):
            region = vbuf.at[c, :, (y + 4 - i) % 4]
            remote(region, region, vy_send.at[i - 1], vy_recv.at[i - 1], sibling).wait_recv()
        vs_copy(c).start()
        vs_copy(1 - c).wait_recv()
        for q in range(2):
            kc[q] = vbuf[0].reshape(PART * BLK, HD)
            vc[q] = vbuf[1].reshape(PART * BLK, HD)

    @pl.when(z < 3)
    def _():
        load_part(0)

    def second(q, _):
        top2, total2, acc2 = attend(q, 0)
        top1 = m_ref[q]
        top = jnp.maximum(top1, top2)
        f1 = jnp.exp2((top1 - top) * FACTOR)
        f2 = jnp.exp2((top2 - top) * FACTOR)
        whole = (f1 * acc_ref[q] + f2 * acc2) / (f1 * l_ref[q] + f2 * total2)
        whole = whole.astype(jnp.bfloat16)
        rows = pl.ds(pl.multiple_of(q * BLK, BLK), BLK)
        for h in range(QH):
            out_ref[rows, h * HD : (h + 1) * HD] = whole[h * BLK : (h + 1) * BLK]
        return 0

    lax.fori_loop(0, 2, second, 0)

    for d in range(3):
        for kv in range(2):

            @pl.when((z_plane(d) <= 7) & jnp.logical_not(z_self(kv, d)))
            def _():
                z_copy(kv, d).wait_send()

    for hi in range(3):
        for kv in range(2):
            for i in range(1, 4):

                @pl.when(p1_live(kv, hi, i))
                def _():
                    p1_copy(kv, hi, i).wait_send()

                @pl.when(p2_live(kv, hi, i))
                def _():
                    p2_copy(kv, hi, i).wait_send()

            for g in range(4):

                @pl.when(needed(hi, g, x))
                def _():
                    sib_copy(kv, hi, g).wait_send()

    @pl.when(z == 2)
    def _():
        for i in range(5):
            vz_copy(i).wait_send()

    @pl.when(z >= 3)
    def _():
        for i in range(1, 4):
            vx_copy(i).wait_send()
            vy_copy(i).wait_send()
        vs_copy(c).wait_send()


def local_attention(queries, key_cache, value_cache, block_list, block_count):
    dma = pltpu.SemaphoreType.DMA
    rows = queries.shape[0] // 4
    return pl.pallas_call(
        attention_kernel,
        out_shape=jax.ShapeDtypeStruct((rows, QH * HD), jnp.bfloat16),
        in_specs=[
            pl.BlockSpec(memory_space=pltpu.SMEM),
            pl.BlockSpec(memory_space=pltpu.SMEM),
            pl.BlockSpec(memory_space=pl.ANY),
            pl.BlockSpec(memory_space=pl.ANY),
            pl.BlockSpec(memory_space=pl.ANY),
        ],
        out_specs=pl.BlockSpec(memory_space=pltpu.VMEM),
        scratch_shapes=[
            pltpu.VMEM((2, 3, 4, 4, 2, 2, BLK, HD), jnp.bfloat16),
            pltpu.VMEM((2, 4, 4, BLK, HD), jnp.bfloat16),
            pltpu.VMEM((2 * BLK, QH * HD), jnp.bfloat16),
            pltpu.VMEM((2, PART * BLK, HD), jnp.bfloat16),
            pltpu.VMEM((2, PART * BLK, HD), jnp.bfloat16),
            pltpu.VMEM((QH * BLK, PART * BLK), jnp.float32),
            pltpu.VMEM((2, QH * BLK, HD), jnp.float32),
            pltpu.VMEM((2, QH * BLK, HD), jnp.float32),
            pltpu.VMEM((2, QH * BLK, HD), jnp.float32),
            dma,
            dma((2, 3)), dma((2, 3)),
            dma((2, 3, 3)), dma((2, 3, 3)),
            dma((2, 3, 3)), dma((2, 3, 3)),
            dma((2, 3, 4)), dma((2, 3, 4)),
            dma((5,)), dma,
            dma((3,)), dma((3,)),
            dma((3,)), dma((3,)),
            dma, dma,
        ],
        compiler_params=pltpu.CompilerParams(has_side_effects=True, vmem_limit_bytes=44 * 1024 * 1024),
    )(block_list, block_count, queries, key_cache.reshape(2, BLK, HD), value_cache.reshape(2, BLK, HD))


def solution(mesh):
    placed = (P("pb", None), P(("ka", "pb"), None), P(("ka", "pb"), None), P("pb", None), P("pb"))
    return jax.shard_map(
        local_attention, mesh=mesh, in_specs=placed, out_specs=P(("pb", "ka"), None), check_vma=False
    )
```

time: 494 us -> 115 us (0.23)
  the two profiles are of different devices: /device:TPU:95 before, /device:TPU:193 now
where the time goes in v1:
time: 115 us
  Pallas kernels  110 us (96%)
  local copies, waits for them, and re-layouts  4.95 us (4%)
    pallas_call x1, Pallas kernels, local_attention(): pl.pallas_call(attention_kernel, out_shape=jax.ShapeDtypeStruct((rows, QH...  110 us
    unnamed x11, local copies, waits for them, and re-layouts  4.95 us

profile of v1, /device:TPU:193, one launch (start us, length us, event | category | flops | bytes accessed | tf_op | source)
XLA Modules:
  0.0 114.9 jit_solution(6017954334557804060)
XLA Ops:
  0.0 0.0 copy-start.4
  0.0 0.7 copy-done.4
  0.7 0.0 copy-start
  0.7 1.2 %copy-done = bf16[1024,512]{1,0:T(8,128)(2,1)S(1)} copy-done((bf16[1024,512]{1,0:T(8,128)(2,1)S(1)}, bf16[1024,512]{1,0:T(8,128)(2,1)}, u32[]{:S(2)}) %copy-start) | copy-done | bytes 1048600
  1.9 0.0 copy-start.1
  1.9 0.8 copy-done.1
  2.7 0.0 copy-start.2
  2.7 0.8 copy-done.2
  3.6 0.0 copy-start.3
  3.6 0.7 copy-done.3
  4.2 109.9 %shard_map.55 = bf16[256,512]{1,0:T(8,128)(2,1)S(1)} custom-call(s32[8,32]{1,0:T(8,128)S(1)} %copy-done.3, s32[8]{0:T(128)S(1)} %copy-done.4, bf16[1024,512]{1,0:T(8,128)(2,1)S(1)} %copy-done, bf16[2,128,128]{2,1,0:T(8,128)(2,1)S(1)} %bitcast.2, bf16[2,128,128]{2,1,0:T(8,128)(2,1)S(1)} %bitcast.3), custom_call_target="tpu_custom_call" | custom-call | tf_op jit(solution)/shard_map/pallas_call | solution.py:356
  114.2 0.7 copy.7
Async XLA Ops:
  0.0 0.7 copy-start.4
  0.7 1.2 %copy-start = (bf16[1024,512]{1,0:T(8,128)(2,1)S(1)}, bf16[1024,512]{1,0:T(8,128)(2,1)}, u32[]{:S(2)}) copy-start(bf16[1024,512]{1,0:T(8,128)(2,1)} %q_hbm.1) | copy-start | bytes 3145732
  1.9 0.8 copy-start.1
  2.7 0.8 copy-start.2
  3.6 0.7 copy-start.3

commit v2 on v1

v2 whole, which is shorter than its diff:
```python
import functools
import math

import jax
import jax.numpy as jnp
from jax import lax
from jax.experimental import pallas as pl
from jax.experimental.pallas import tpu as pltpu
from jax.sharding import PartitionSpec as P

HD = 128
QH = 4
BLK = 128
LIST = 32
NV = 16
PART = 16
CHUNK = 4
MASKED = -1e30
FACTOR = math.log2(math.e) / math.sqrt(HD)


def attention_kernel(
    list_hbm, count_hbm, q_hbm, k_hbm, v_hbm, out_ref,
    list_ref, count_ref, pick_ref,
    buf, vbuf, qs, kc, vc, s_ref, acc_ref, m_ref, l_ref, part_out, part_in, half_out, half_in,
    in_sem, z_send, z_recv, f_send, p1_send, p1_recv, p2_send, p2_recv, sib_send, sib_recv,
    vp_send, vp_recv, vh_send, vh_recv, vz_send, vz_recv, v1_send, v1_recv, v2_send, v2_recv, vs_send, vs_recv,
):
    p = lax.axis_index("pb")
    y = lax.axis_index("ka")
    z = p // 8
    x = (p // 2) % 4
    c = p % 2

    def dev(zz, xx, cc, yy):
        return (zz * 8 + xx * 2 + cc, yy)

    def remote(src, dst, ssem, rsem, device):
        return pltpu.make_async_remote_copy(
            src_ref=src, dst_ref=dst, send_sem=ssem, recv_sem=rsem,
            device_id=device, device_id_type=pl.DeviceIdType.MESH,
        )

    def have(hi):
        return z >= 2 - hi

    def needed(hi, g, xx):
        if hi == 1:
            return have(hi)
        if hi == 0:
            return have(hi) & (g >= xx)
        return g <= xx

    inputs = [
        pltpu.make_async_copy(list_hbm, list_ref, in_sem.at[0]),
        pltpu.make_async_copy(count_hbm, count_ref, in_sem.at[1]),
        pltpu.make_async_copy(q_hbm.at[pl.ds(pl.multiple_of(y * 256, 256), 256)], qs, in_sem.at[2]),
    ]
    for copy in inputs:
        copy.start()

    src = (k_hbm, v_hbm)
    g_own = z % 4
    half = 2 * y + z // 4
    z_plane = jnp.minimum(half + 1, 7)
    z_half = jnp.where(half == 7, 2, 1)

    def z_target(kv):
        xd, yd = (x, g_own) if kv == 0 else (g_own, x)
        return z_plane, xd, c, yd

    def z_source(kv, h):
        return (4 * (h % 2) + y, x, c, h // 2) if kv == 0 else (4 * (h % 2) + x, y, c, h // 2)

    def here(device):
        zz, xx, _, yy = device
        return (zz == z) & (xx == x) & (yy == y)

    barrier = pltpu.get_barrier_semaphore()
    partners = []
    always = z >= 0
    for i in range(1, 4):
        partners.append((always, (z, (x + i) % 4, c, y)))
        partners.append((always, (z, x, c, (y + i) % 4)))
    partners.append((always, (z, x, 1 - c, y)))
    partners.append((z >= 1, (jnp.maximum(z - 1, 0), x, c, y)))
    partners.append((z <= 6, (jnp.minimum(z + 1, 7), x, c, y)))
    for i in range(5):
        partners.append((z == 2, (3 + i, x, c, y)))
    partners.append((z >= 3, (2, x, c, y)))
    for kv in range(2):
        there = z_target(kv)
        partners.append((jnp.logical_not(here(there)), there))
        there = z_source(kv, jnp.maximum(z - 1, 0))
        partners.append(((z >= 1) & jnp.logical_not(here(there)), there))
        there = z_source(kv, 7)
        partners.append(((z == 7) & jnp.logical_not(here(there)), there))
    expected = jnp.int32(0)
    for live, there in partners:

        @pl.when(live)
        def _():
            pl.semaphore_signal(barrier, inc=1, device_id=dev(*there), device_id_type=pl.DeviceIdType.MESH)

        expected = expected + jnp.where(live, 1, 0)
    pl.semaphore_wait(barrier, expected)

    def z_copy(kv):
        region = buf.at[kv, z_half, g_own, x, c]
        return remote(src[kv], region, z_send.at[kv], z_recv.at[kv, z_half], dev(*z_target(kv)))

    for kv in range(2):
        own = here(z_target(kv))

        @pl.when(jnp.logical_not(own))
        def _():
            z_copy(kv).start()

        @pl.when(own)
        def _():
            pltpu.make_async_copy(src[kv], buf.at[kv, z_half, g_own, x, c], z_recv.at[kv, z_half]).start()

    def row(kv):
        return y if kv == 0 else x

    def col(kv):
        return x if kv == 0 else y

    def along(kv, i):
        return dev(z, (x + i) % 4, c, y) if kv == 0 else dev(z, x, c, (y + i) % 4)

    def across(kv, i):
        return dev(z, x, c, (y + i) % 4) if kv == 0 else dev(z, (x + i) % 4, c, y)

    sibling = dev(z, x, 1 - c, y)

    def p1_copy(kv, hi, i):
        region = buf.at[kv, hi, row(kv), col(kv), c]
        return remote(region, region, p1_send.at[kv, hi, i - 1], p1_recv.at[kv, hi, i - 1], along(kv, i))

    def p1_live(kv, hi, i):
        if kv == 1:
            return have(hi)
        wanted = needed(hi, y, (x + i) % 4)
        return wanted | (z == 2) if hi == 0 else wanted

    def p1_got(kv, hi):
        if kv == 1:
            return have(hi)
        wanted = needed(hi, y, x)
        return wanted | (z == 2) if hi == 0 else wanted

    def p2_copy(kv, hi, i):
        region = buf.at[kv, hi, row(kv), :, c]
        return remote(region, region, p2_send.at[kv, hi, i - 1], p2_recv.at[kv, hi, i - 1], across(kv, i))

    def p2_live(kv, hi, i):
        return needed(hi, y, x) if kv == 0 else needed(hi, x, (x + i) % 4)

    def sib_copy(kv, hi, g):
        region = buf.at[kv, hi, g, :, c]
        return remote(region, region, sib_send.at[kv, hi, g], sib_recv.at[kv, hi, g], sibling)

    def vz_copy(i):
        return remote(vbuf.at[c, x, y], vbuf.at[c, x, y], vz_send.at[i], vz_recv, dev(3 + i, x, c, y))

    def v_line(first, i):
        to_x = (c == 0) == first
        return dev(z, jnp.where(to_x, (x + i) % 4, x), c, jnp.where(to_x, y, (y + i) % 4))

    def v1_copy(i):
        return remote(vbuf.at[c, x, y], vbuf.at[c, x, y], v1_send.at[i - 1], v1_recv.at[i - 1], v_line(True, i))

    def v2_copy(cc, i):
        region = vbuf.at[0, :, y] if cc == 0 else vbuf.at[1, x]
        return remote(region, region, v2_send.at[i - 1], v2_recv.at[i - 1], v_line(False, i))

    def vs_copy(cc):
        return remote(vbuf.at[cc], vbuf.at[cc], vs_send, vs_recv, sibling)

    def f_copy(kv, up):
        region = buf.at[kv, 1, row(kv), col(kv), c]
        there = buf.at[kv, 0 if up else 2, row(kv), col(kv), c]
        to = jnp.minimum(z + 1, 7) if up else jnp.maximum(z - 1, 0)
        return remote(region, there, f_send.at[kv, int(up)], z_recv.at[kv, 0 if up else 2], dev(to, x, c, y))

    def f_live(up):
        return (z >= 1) & (z <= 6) if up else z >= 1

    for copy in inputs[:2]:
        copy.wait()

    @pl.when(z == 2)
    def _():
        entries = [list_ref[2 * y, i] for i in range(NV)]
        slots = [4 * x + (y + i) % 4 for i in range(4)] + [4 * ((x + i) % 4) + y for i in range(4)]
        chosen = [jnp.int32(-1)] * 8
        for i in range(NV):
            rank = jnp.int32(0)
            for j in range(NV):
                if j != i:
                    rank = rank + jnp.where(entries[j] < entries[i], 1, 0)
            chosen = [jnp.where(rank == slot, entries[i], now) for slot, now in zip(slots, chosen)]
        for n in range(8):
            pick_ref[n] = chosen[n]

    for hi in (1, 2, 0):
        for kv in range(2):

            @pl.when(have(hi))
            def _():
                pltpu.make_async_copy(src[kv], buf.at[kv, hi, row(kv), col(kv), c], z_recv.at[kv, hi]).wait()

            if hi == 1:
                for up in (False, True):

                    @pl.when(f_live(up))
                    def _():
                        f_copy(kv, up).start()

            for i in (1, 3, 2):

                @pl.when(p1_live(kv, hi, i))
                def _():
                    p1_copy(kv, hi, i).start()

    def p1_wait(hi):
        for kv in range(2):
            for i in (1, 3, 2):

                @pl.when(p1_got(kv, hi))
                def _():
                    region = buf.at[kv, hi, row(kv), (col(kv) + 4 - i) % 4, c]
                    remote(region, region, p1_send.at[kv, hi, i - 1], p1_recv.at[kv, hi, i - 1], sibling).wait_recv()

    def p2_start(hi, when):
        for kv in range(2):
            for i in (1, 3, 2):

                @pl.when(p2_live(kv, hi, i) & when)
                def _():
                    p2_copy(kv, hi, i).start()

            @pl.when(needed(hi, row(kv), x) & when)
            def _():
                sib_copy(kv, hi, row(kv)).start()

    def collect(hi):
        for i in (1, 3, 2):
            for kv in range(2):
                g = (row(kv) + 4 - i) % 4

                @pl.when(needed(hi, g, x))
                def _():
                    region = buf.at[kv, hi, g, :, c]
                    remote(region, region, p2_send.at[kv, hi, i - 1], p2_recv.at[kv, hi, i - 1], sibling).wait_recv()
                    sib_copy(kv, hi, g).start()

    def vp_copy(kv, i):
        return remote(
            part_out.at[kv, i], part_in.at[kv, i - 1], vp_send.at[kv, i - 1], vp_recv.at[kv, i - 1], across(kv, i)
        )

    def vh_copy(kv):
        return remote(half_out.at[kv], half_in, vh_send, vh_recv, sibling)

    p1_wait(1)
    p2_start(1, z != 2)
    p1_wait(2)
    p1_wait(0)

    @pl.when(z == 2)
    def _():
        for kv in range(2):

            def pick(n, _):
                l, r, hi = n // 4, (n // 2) % 2, n % 2
                block = buf[kv, hi, row(kv), l, c, r]
                name = 64 * hi + 16 * row(kv) + 4 * l + 2 * c + r
                for i in range(4):
                    part_out[kv, i] = jnp.where(pick_ref[4 * kv + i] == name, block, part_out[kv, i])
                return 0

            part_out[kv] = jnp.zeros((4, BLK, HD), jnp.bfloat16)
            lax.fori_loop(0, 16, pick, 0)
            for i in (1, 3, 2):
                vp_copy(kv, i).start()

    p2_start(1, z == 2)
    p2_start(2, z >= 0)

    @pl.when(z == 2)
    def _():
        for kv in range(2):
            for i in (1, 3, 2):
                vp_copy(kv, i).wait_recv()
            half_out[kv] = (part_out[kv, 0] + part_in[kv, 0]) + (part_in[kv, 1] + part_in[kv, 2])
        vh_copy(1 - c).start()
        vh_copy(c).wait_recv()
        vbuf[c, x, y] = half_out[c] + half_in[...]
        for i in (0, 4, 1, 3, 2):
            vz_copy(i).start()

    @pl.when(z >= 3)
    def _():
        vz_copy(0).wait_recv()

    @pl.when(z >= 2)
    def _():
        for i in (1, 3, 2):
            v1_copy(i).start()
        for i in (1, 3, 2):
            v1_copy(i).wait_recv()
        for cc in range(2):

            @pl.when(c == cc)
            def _():
                for i in (1, 3, 2):
                    v2_copy(cc, i).start()

    p2_start(0, z >= 0)
    collect(1)
    collect(2)

    @pl.when(z >= 2)
    def _():
        for cc in range(2):

            @pl.when(c == cc)
            def _():
                for i in (1, 3, 2):
                    v2_copy(cc, i).wait_recv()
                vs_copy(cc).start()
                vs_copy(1 - cc).wait_recv()

    def place(block):
        rel = jnp.clip(block - 64 * (z - 2), 0, 191)
        return rel >> 6, (rel >> 4) & 3, (rel >> 2) & 3, (rel >> 1) & 1, rel & 1

    def block_of(kv, block):
        hi, g, l, cc, r = place(block)
        return buf[kv, hi, g, l, cc, r]

    delta = lax.broadcasted_iota(jnp.int32, (BLK, BLK), 1) - lax.broadcasted_iota(jnp.int32, (BLK, BLK), 0)

    def load_part(part):
        def load(n, _):
            q = n // PART
            s = n % PART
            block = list_ref[2 * y + q, part * PART + s]
            rows = pl.ds(pl.multiple_of(s * BLK, BLK), BLK)
            kc[q, rows, :] = block_of(0, block)
            vc[q, rows, :] = block_of(1, block)
            return 0

        lax.fori_loop(0, 2 * PART, load, 0)

    def keys_of(q, part, masked, n):
        if masked:
            return kc[q, n * CHUNK * BLK : (n + 1) * CHUNK * BLK, :]
        return vbuf[0, n].reshape(CHUNK * BLK, HD)

    def values_of(q, part, masked, n):
        if masked:
            return vc[q, n * CHUNK * BLK : (n + 1) * CHUNK * BLK, :]
        return vbuf[1, n].reshape(CHUNK * BLK, HD)

    def attend(q, part, masked=True):
        my_block = 8 * p + 2 * y + q
        count = count_ref[2 * y + q]
        rows = pl.ds(pl.multiple_of(q * BLK, BLK), BLK)
        q4 = jnp.concatenate([qs[rows, h * HD : (h + 1) * HD] for h in range(QH)], axis=0)
        width = CHUNK * BLK
        peak = None
        for n in range(PART // CHUNK):
            keys = keys_of(q, part, masked, n)
            scores = lax.dot_general(q4, keys, (((1,), (1,)), ((), ())), preferred_element_type=jnp.float32)
            for k in range(CHUNK):
                if not masked:
                    tile = scores[:, k * BLK : (k + 1) * BLK]
                    peak = tile if peak is None else jnp.maximum(peak, tile)
                    continue
                slot = part * PART + n * CHUNK + k
                block = list_ref[2 * y + q, slot]
                reach = jnp.where(block == my_block, 0, BLK)
                reach = jnp.where(slot < count, reach, -BLK)
                ok = delta <= reach
                tile = scores[:, k * BLK : (k + 1) * BLK].reshape(QH, BLK, BLK)
                tile = jnp.where(ok[None], tile, MASKED).reshape(QH * BLK, BLK)
                s_ref[:, (n * CHUNK + k) * BLK : (n * CHUNK + k + 1) * BLK] = tile
                peak = tile if peak is None else jnp.maximum(peak, tile)
            if not masked:
                s_ref[:, n * width : (n + 1) * width] = scores
        top = jnp.max(peak, axis=1, keepdims=True)
        total = None
        acc = None
        for n in range(PART // CHUNK):
            weights = jnp.exp2((s_ref[:, n * width : (n + 1) * width] - top) * FACTOR)
            for k in range(CHUNK):
                tile = weights[:, k * BLK : (k + 1) * BLK]
                total = tile if total is None else total + tile
            values = values_of(q, part, masked, n)
            out = jnp.dot(weights.astype(jnp.bfloat16), values, preferred_element_type=jnp.float32)
            acc = out if acc is None else acc + out
        return top, jnp.sum(total, axis=1, keepdims=True), acc

    def first(q, masked):
        top, total, acc = attend(q, 0, masked)
        acc_ref[q] = acc
        m_ref[q] = jnp.broadcast_to(top, (QH * BLK, HD))
        l_ref[q] = jnp.broadcast_to(total, (QH * BLK, HD))

    inputs[2].wait()

    @pl.when(z >= 2)
    def _():
        def early(q, _):
            first(q, False)
            return 0

        lax.fori_loop(0, 2, early, 0)

    collect(0)
    for hi in (1, 2, 0):
        for kv in range(2):
            for g in range(4):

                @pl.when(needed(hi, g, x))
                def _():
                    region = buf.at[kv, hi, g, :, 1 - c]
                    remote(region, region, sib_send.at[kv, hi, g], sib_recv.at[kv, hi, g], sibling).wait_recv()

    @pl.when(z < 2)
    def _():
        load_part(0)

        def late(q, _):
            first(q, True)
            return 0

        lax.fori_loop(0, 2, late, 0)

    load_part(1)

    def second(q, _):
        top2, total2, acc2 = attend(q, 1)
        top1 = m_ref[q]
        top = jnp.maximum(top1, top2)
        f1 = jnp.exp2((top1 - top) * FACTOR)
        f2 = jnp.exp2((top2 - top) * FACTOR)
        whole = (f1 * acc_ref[q] + f2 * acc2) / (f1 * l_ref[q] + f2 * total2)
        whole = whole.astype(jnp.bfloat16)
        rows = pl.ds(pl.multiple_of(q * BLK, BLK), BLK)
        for h in range(QH):
            out_ref[rows, h * HD : (h + 1) * HD] = whole[h * BLK : (h + 1) * BLK]
        return 0

    lax.fori_loop(0, 2, second, 0)

    for kv in range(2):

        @pl.when(jnp.logical_not(here(z_target(kv))))
        def _():
            z_copy(kv).wait_send()

        for up in (False, True):

            @pl.when(f_live(up))
            def _():
                f_copy(kv, up).wait_send()

    for hi in range(3):
        for kv in range(2):
            for i in range(1, 4):

                @pl.when(p1_live(kv, hi, i))
                def _():
                    p1_copy(kv, hi, i).wait_send()

                @pl.when(p2_live(kv, hi, i))
                def _():
                    p2_copy(kv, hi, i).wait_send()

            for g in range(4):

                @pl.when(needed(hi, g, x))
                def _():
                    sib_copy(kv, hi, g).wait_send()

    @pl.when(z == 2)
    def _():
        for kv in range(2):
            for i in range(1, 4):
                vp_copy(kv, i).wait_send()
        vh_copy(1 - c).wait_send()
        for i in range(5):
            vz_copy(i).wait_send()

    @pl.when(z >= 2)
    def _():
        for i in range(1, 4):
            v1_copy(i).wait_send()
        for cc in range(2):

            @pl.when(c == cc)
            def _():
                for i in range(1, 4):
                    v2_copy(cc, i).wait_send()
                vs_copy(cc).wait_send()


def local_attention(queries, key_cache, value_cache, block_list, block_count):
    dma = pltpu.SemaphoreType.DMA
    rows = queries.shape[0] // 4
    return pl.pallas_call(
        attention_kernel,
        out_shape=jax.ShapeDtypeStruct((rows, QH * HD), jnp.bfloat16),
        in_specs=[
            pl.BlockSpec(memory_space=pl.ANY),
            pl.BlockSpec(memory_space=pl.ANY),
            pl.BlockSpec(memory_space=pl.ANY),
            pl.BlockSpec(memory_space=pl.ANY),
            pl.BlockSpec(memory_space=pl.ANY),
        ],
        out_specs=pl.BlockSpec(memory_space=pltpu.VMEM),
        scratch_shapes=[
            pltpu.SMEM((8, LIST), jnp.int32),
            pltpu.SMEM((8,), jnp.int32),
            pltpu.SMEM((8,), jnp.int32),
            pltpu.VMEM((2, 3, 4, 4, 2, 2, BLK, HD), jnp.bfloat16),
            pltpu.VMEM((2, 4, 4, BLK, HD), jnp.bfloat16),
            pltpu.VMEM((2 * BLK, QH * HD), jnp.bfloat16),
            pltpu.VMEM((2, PART * BLK, HD), jnp.bfloat16),
            pltpu.VMEM((2, PART * BLK, HD), jnp.bfloat16),
            pltpu.VMEM((QH * BLK, PART * BLK), jnp.float32),
            pltpu.VMEM((2, QH * BLK, HD), jnp.float32),
            pltpu.VMEM((2, QH * BLK, HD), jnp.float32),
            pltpu.VMEM((2, QH * BLK, HD), jnp.float32),
            pltpu.VMEM((2, 4, BLK, HD), jnp.bfloat16),
            pltpu.VMEM((2, 3, BLK, HD), jnp.bfloat16),
            pltpu.VMEM((2, BLK, HD), jnp.bfloat16),
            pltpu.VMEM((BLK, HD), jnp.bfloat16),
            dma((3,)),
            dma((2,)), dma((2, 3)), dma((2, 2)),
            dma((2, 3, 3)), dma((2, 3, 3)),
            dma((2, 3, 3)), dma((2, 3, 3)),
            dma((2, 3, 4)), dma((2, 3, 4)),
            dma((2, 3)), dma((2, 3)),
            dma, dma,
            dma((5,)), dma,
            dma((3,)), dma((3,)),
            dma((3,)), dma((3,)),
            dma, dma,
        ],
        compiler_params=pltpu.CompilerParams(collective_id=0, has_side_effects=True, vmem_limit_bytes=60 * 1024 * 1024),
    )(block_list, block_count, queries, key_cache.reshape(2, BLK, HD), value_cache.reshape(2, BLK, HD))


def solution(mesh):
    placed = (P("pb", None), P(("ka", "pb"), None), P(("ka", "pb"), None), P("pb", None), P("pb"))
    return jax.shard_map(
        local_attention, mesh=mesh, in_specs=placed, out_specs=P(("pb", "ka"), None), check_vma=False
    )
```

time: 115 us -> 88.1 us (0.77)
  the two profiles are of different devices: /device:TPU:193 before, /device:TPU:89 now
where the time goes in v2:
time: 88.1 us; the launch traced here: 87.9 us
  Pallas kernels  86.3 us (98%)
  local copies, waits for them, and re-layouts  1.67 us (2%)
    pallas_call x1, Pallas kernels, local_attention(): pl.pallas_call(attention_kernel, out_shape=jax.ShapeDtypeStruct((rows, QH...  86.3 us

profile of v2, /device:TPU:89, one launch (start us, length us, event | category | flops | bytes accessed | tf_op | source)
XLA Modules:
  0.0 87.9 jit_solution(17841732365238840488)
XLA Ops:
  0.0 86.3 %shard_map.55 = bf16[256,512]{1,0:T(8,128)(2,1)} custom-call(s32[8,32]{1,0:T(8,128)} %list_hbm.1, s32[8]{0:T(128)} %count_hbm.1, bf16[1024,512]{1,0:T(8,128)(2,1)} %q_hbm.1, bf16[2,128,128]{2,1,0:T(8,128)(2,1)} %bitcast.2, bf16[2,128,128]{2,1,0:T(8,128)(2,1)} %bitcast.3), custom_call_target="tpu_custom_call" | custom-call | tf_op jit(solution)/shard_map/pallas_call | solution.py:515
  86.3 1.7 %copy.7 = bf16[256,512]{1,0:T(8,128)(2,1)} copy(bf16[256,512]{1,0:T(8,128)(2,1)} %shard_map.55) | data formatting | bytes 524288

commit v3 on v2

--- a/solution.py
+++ b/solution.py
@@ -23,7 +23,7 @@
     list_hbm, count_hbm, q_hbm, k_hbm, v_hbm, out_ref,
     list_ref, count_ref, pick_ref,
     buf, vbuf, qs, kc, vc, s_ref, acc_ref, m_ref, l_ref, part_out, part_in, half_out, half_in,
-    in_sem, z_send, z_recv, f_send, p1_send, p1_recv, p2_send, p2_recv, sib_send, sib_recv,
+    in_sem, z_send, z_recv, f_send, p1_send, p1_recv, p2_send, p2_recv, f2_send, f2_recv, sib_send, sib_recv,
     vp_send, vp_recv, vh_send, vh_recv, vz_send, vz_recv, v1_send, v1_recv, v2_send, v2_recv, vs_send, vs_recv,
 ):
     p = lax.axis_index("pb")
@@ -154,6 +154,14 @@
         region = buf.at[kv, hi, row(kv), :, c]
         return remote(region, region, p2_send.at[kv, hi, i - 1], p2_recv.at[kv, hi, i - 1], across(kv, i))
 
+    def relayed(kv, hi):
+        return kv == 0 or hi == 1
+
+    def far_copy(kv, hi, i):
+        g, first = (row(kv) + 4 - i) % 4, 0 if i == 1 else 2
+        region = buf.at[kv, hi, g, first : first + 2, c]
+        return remote(region, region, f2_send.at[kv, hi, i // 2], f2_recv.at[kv, hi, i // 2], across(kv, i))
+
     def p2_live(kv, hi, i):
         return needed(hi, y, x) if kv == 0 else needed(hi, x, (x + i) % 4)
 
@@ -204,7 +212,7 @@
         for n in range(8):
             pick_ref[n] = chosen[n]
 
-    for hi in (1, 2, 0):
+    for hi in (1, 0, 2):
         for kv in range(2):
 
             @pl.when(have(hi))
@@ -235,7 +243,7 @@
 
     def p2_start(hi, when):
         for kv in range(2):
-            for i in (1, 3, 2):
+            for i in (1, 3) if relayed(kv, hi) else (1, 3, 2):
 
                 @pl.when(p2_live(kv, hi, i) & when)
                 def _():
@@ -245,8 +253,8 @@
             def _():
                 sib_copy(kv, hi, row(kv)).start()
 
-    def collect(hi):
-        for i in (1, 3, 2):
+    def near(hi):
+        for i in (1, 3):
             for kv in range(2):
                 g = (row(kv) + 4 - i) % 4
 
@@ -254,7 +262,25 @@
                 def _():
                     region = buf.at[kv, hi, g, :, c]
                     remote(region, region, p2_send.at[kv, hi, i - 1], p2_recv.at[kv, hi, i - 1], sibling).wait_recv()
+                    if relayed(kv, hi):
+                        far_copy(kv, hi, i).start()
                     sib_copy(kv, hi, g).start()
+
+    def far(hi):
+        for kv in range(2):
+            g = (row(kv) + 2) % 4
+
+            @pl.when(needed(hi, g, x))
+            def _():
+                if relayed(kv, hi):
+                    for i in (1, 3):
+                        first = 0 if i == 1 else 2
+                        region = buf.at[kv, hi, g, first : first + 2, c]
+                        remote(region, region, f2_send.at[kv, hi, i // 2], f2_recv.at[kv, hi, i // 2], sibling).wait_recv()
+                else:
+                    region = buf.at[kv, hi, g, :, c]
+                    remote(region, region, p2_send.at[kv, hi, 1], p2_recv.at[kv, hi, 1], sibling).wait_recv()
+                sib_copy(kv, hi, g).start()
 
     def vp_copy(kv, i):
         return remote(
@@ -265,28 +291,27 @@
         return remote(half_out.at[kv], half_in, vh_send, vh_recv, sibling)
 
     p1_wait(1)
-    p2_start(1, z != 2)
-    p1_wait(2)
+    p2_start(1, z >= 0)
     p1_wait(0)
 
     @pl.when(z == 2)
     def _():
         for kv in range(2):
 
-            def pick(n, _):
-                l, r, hi = n // 4, (n // 2) % 2, n % 2
-                block = buf[kv, hi, row(kv), l, c, r]
-                name = 64 * hi + 16 * row(kv) + 4 * l + 2 * c + r
-                for i in range(4):
-                    part_out[kv, i] = jnp.where(pick_ref[4 * kv + i] == name, block, part_out[kv, i])
-                return 0
-
-            part_out[kv] = jnp.zeros((4, BLK, HD), jnp.bfloat16)
-            lax.fori_loop(0, 16, pick, 0)
+            picked = [jnp.zeros((BLK, HD), jnp.bfloat16)] * 4
+            for hi in range(2):
+                for l in range(4):
+                    for r in range(2):
+                        block = buf[kv, hi, row(kv), l, c, r]
+                        name = 64 * hi + 16 * row(kv) + 4 * l + 2 * c + r
+                        picked = [jnp.where(pick_ref[4 * kv + i] == name, block, picked[i]) for i in range(4)]
+            for i in range(4):
+                part_out[kv, i] = picked[i]
             for i in (1, 3, 2):
                 vp_copy(kv, i).start()
 
-    p2_start(1, z == 2)
+    p2_start(0, z >= 0)
+    p1_wait(2)
     p2_start(2, z >= 0)
 
     @pl.when(z == 2)
@@ -301,6 +326,9 @@
         for i in (0, 4, 1, 3, 2):
             vz_copy(i).start()
 
+    near(1)
+    near(0)
+
     @pl.when(z >= 3)
     def _():
         vz_copy(0).wait_recv()
@@ -309,6 +337,12 @@
     def _():
         for i in (1, 3, 2):
             v1_copy(i).start()
+
+    far(1)
+    near(2)
+
+    @pl.when(z >= 2)
+    def _():
         for i in (1, 3, 2):
             v1_copy(i).wait_recv()
         for cc in range(2):
@@ -318,20 +352,16 @@
                 for i in (1, 3, 2):
                     v2_copy(cc, i).start()
 
-    p2_start(0, z >= 0)
-    collect(1)
-    collect(2)
-
-    @pl.when(z >= 2)
-    def _():
-        for cc in range(2):
-
-            @pl.when(c == cc)
-            def _():
-                for i in (1, 3, 2):
-                    v2_copy(cc, i).wait_recv()
-                vs_copy(cc).start()
-                vs_copy(1 - cc).wait_recv()
+    far(0)
+    far(2)
+    for hi in (1, 0, 2):
+        for kv in range(2):
+            for g in range(4):
+
+                @pl.when(needed(hi, g, x))
+                def _():
+                    region = buf.at[kv, hi, g, :, 1 - c]
+                    remote(region, region, sib_send.at[kv, hi, g], sib_recv.at[kv, hi, g], sibling).wait_recv()
 
     def place(block):
         rel = jnp.clip(block - 64 * (z - 2), 0, 191)
@@ -404,46 +434,32 @@
             acc = out if acc is None else acc + out
         return top, jnp.sum(total, axis=1, keepdims=True), acc
 
-    def first(q, masked):
-        top, total, acc = attend(q, 0, masked)
+    inputs[2].wait()
+    load_part(1)
+
+    def first(q, _):
+        top, total, acc = attend(q, 1)
         acc_ref[q] = acc
         m_ref[q] = jnp.broadcast_to(top, (QH * BLK, HD))
         l_ref[q] = jnp.broadcast_to(total, (QH * BLK, HD))
-
-    inputs[2].wait()
+        return 0
+
+    lax.fori_loop(0, 1, first, 0)
 
     @pl.when(z >= 2)
     def _():
-        def early(q, _):
-            first(q, False)
-            return 0
-
-        lax.fori_loop(0, 2, early, 0)
-
-    collect(0)
-    for hi in (1, 2, 0):
-        for kv in range(2):
-            for g in range(4):
-
-                @pl.when(needed(hi, g, x))
-                def _():
-                    region = buf.at[kv, hi, g, :, 1 - c]
-                    remote(region, region, sib_send.at[kv, hi, g], sib_recv.at[kv, hi, g], sibling).wait_recv()
-
-    @pl.when(z < 2)
-    def _():
-        load_part(0)
-
-        def late(q, _):
-            first(q, True)
-            return 0
-
-        lax.fori_loop(0, 2, late, 0)
-
-    load_part(1)
-
-    def second(q, _):
-        top2, total2, acc2 = attend(q, 1)
+        for cc in range(2):
+
+            @pl.when(c == cc)
+            def _():
+                for i in (1, 3, 2):
+                    v2_copy(cc, i).wait_recv()
+                vs_copy(cc).start()
+
+    lax.fori_loop(1, 2, first, 0)
+
+    def second(q, masked):
+        top2, total2, acc2 = attend(q, 0, masked)
         top1 = m_ref[q]
         top = jnp.maximum(top1, top2)
         f1 = jnp.exp2((top1 - top) * FACTOR)
@@ -453,9 +469,26 @@
         rows = pl.ds(pl.multiple_of(q * BLK, BLK), BLK)
         for h in range(QH):
             out_ref[rows, h * HD : (h + 1) * HD] = whole[h * BLK : (h + 1) * BLK]
-        return 0
-
-    lax.fori_loop(0, 2, second, 0)
+
+    @pl.when(z >= 2)
+    def _():
+        vs_copy(1 - c).wait_recv()
+
+        def gathered(q, _):
+            second(q, False)
+            return 0
+
+        lax.fori_loop(0, 2, gathered, 0)
+
+    @pl.when(z < 2)
+    def _():
+        load_part(0)
+
+        def windowed(q, _):
+            second(q, True)
+            return 0
+
+        lax.fori_loop(0, 2, windowed, 0)
 
     for kv in range(2):
 
@@ -477,9 +510,18 @@
                 def _():
                     p1_copy(kv, hi, i).wait_send()
 
+                if i == 2 and relayed(kv, hi):
+                    continue
+
                 @pl.when(p2_live(kv, hi, i))
                 def _():
                     p2_copy(kv, hi, i).wait_send()
+
+            for i in (1, 3) if relayed(kv, hi) else ():
+
+                @pl.when(needed(hi, (row(kv) + 4 - i) % 4, x))
+                def _():
+                    far_copy(kv, hi, i).wait_send()
 
             for g in range(4):
 
@@ -544,6 +586,7 @@
             dma((2,)), dma((2, 3)), dma((2, 2)),
             dma((2, 3, 3)), dma((2, 3, 3)),
             dma((2, 3, 3)), dma((2, 3, 3)),
+            dma((2, 3, 2)), dma((2, 3, 2)),
             dma((2, 3, 4)), dma((2, 3, 4)),
             dma((2, 3)), dma((2, 3)),
             dma, dma,

time: 88.1 us -> 72.8 us (0.83)
  the two profiles are of different devices: /device:TPU:89 before, /device:TPU:95 now
where the time goes in v3:
time: 72.8 us; the launch traced here: 72.6 us
  Pallas kernels  71 us (98%)
  local copies, waits for them, and re-layouts  1.67 us (2%)
    pallas_call x1, Pallas kernels, local_attention(): pl.pallas_call(attention_kernel, out_shape=jax.ShapeDtypeStruct((rows, QH...  71 us
    unnamed x1, local copies, waits for them, and re-layouts  1.67 us

profile of v3, /device:TPU:95, one launch (start us, length us, event | category | flops | bytes accessed | tf_op | source)
XLA Modules:
  0.0 72.6 jit_solution(2623532525079563943)
XLA Ops:
  0.0 71.0 %shard_map.55 = bf16[256,512]{1,0:T(8,128)(2,1)} custom-call(s32[8,32]{1,0:T(8,128)} %list_hbm.1, s32[8]{0:T(128)} %count_hbm.1, bf16[1024,512]{1,0:T(8,128)(2,1)} %q_hbm.1, bf16[2,128,128]{2,1,0:T(8,128)(2,1)} %bitcast.2, bf16[2,128,128]{2,1,0:T(8,128)(2,1)} %bitcast.3), custom_call_target="tpu_custom_call" | custom-call | tf_op jit(solution)/shard_map/pallas_call | solution.py:557
  71.0 1.7 %copy.7 = bf16[256,512]{1,0:T(8,128)(2,1)} copy(bf16[256,512]{1,0:T(8,128)(2,1)} %shard_map.55) | data formatting | bytes 524288

commit v4 on v3

--- a/solution.py
+++ b/solution.py
@@ -22,7 +22,7 @@
 def attention_kernel(
     list_hbm, count_hbm, q_hbm, k_hbm, v_hbm, out_ref,
     list_ref, count_ref, pick_ref,
-    buf, vbuf, qs, kc, vc, s_ref, acc_ref, m_ref, l_ref, part_out, part_in, half_out, half_in,
+    buf, vbuf, qs, kc, vc, s_ref, acc_ref, m_ref, part_out, part_in, half_out, half_in,
     in_sem, z_send, z_recv, f_send, p1_send, p1_recv, p2_send, p2_recv, f2_send, f2_recv, sib_send, sib_recv,
     vp_send, vp_recv, vh_send, vh_recv, vz_send, vz_recv, v1_send, v1_recv, v2_send, v2_recv, vs_send, vs_recv,
 ):
@@ -373,11 +373,80 @@
 
     delta = lax.broadcasted_iota(jnp.int32, (BLK, BLK), 1) - lax.broadcasted_iota(jnp.int32, (BLK, BLK), 0)
 
-    def load_part(part):
+    ones = jnp.ones((CHUNK * BLK, HD), jnp.bfloat16)
+    second_set = jnp.where(z >= 2, 0, 1)
+
+    def keys_of(kv, q, part, n):
+        if part == 1:
+            return jnp.concatenate(
+                [block_of(kv, list_ref[2 * y + q, PART + n * CHUNK + k]) for k in range(CHUNK)], axis=0
+            )
+        held = kc if kv == 0 else vc
+        return held[q * second_set, n * CHUNK * BLK : (n + 1) * CHUNK * BLK, :]
+
+    queries_of = []
+
+    def score_chunk(q, part, n, peak):
+        my_block = 8 * p + 2 * y + q
+        count = count_ref[2 * y + q]
+        scores = lax.dot_general(
+            queries_of[q], keys_of(0, q, part, n), (((1,), (1,)), ((), ())), preferred_element_type=jnp.float32
+        )
+        for k in range(CHUNK):
+            slot = part * PART + n * CHUNK + k
+            block = list_ref[2 * y + q, slot]
+            reach = jnp.where(block == my_block, 0, BLK)
+            reach = jnp.where(slot < count, reach, -BLK)
+            ok = delta <= reach
+            tile = scores[:, k * BLK : (k + 1) * BLK].reshape(QH, BLK, BLK)
+            tile = jnp.where(ok[None], tile, MASKED).reshape(QH * BLK, BLK)
+            s_ref[q, :, (n * CHUNK + k) * BLK : (n * CHUNK + k + 1) * BLK] = tile
+            peak = tile if peak is None else jnp.maximum(peak, tile)
+        return peak
+
+    def apply_chunk(q, part, n, top, acc):
+        scores = s_ref[q, :, n * CHUNK * BLK : (n + 1) * CHUNK * BLK]
+        weights = jnp.exp2((scores - top) * FACTOR).astype(jnp.bfloat16)
+        values = jnp.concatenate([keys_of(1, q, part, n), ones], axis=1)
+        out = jnp.dot(weights, values, preferred_element_type=jnp.float32)
+        return out if acc is None else acc + out
+
+    def stage(scored, applied, top):
+        peak = acc = None
+        for n in range(PART // CHUNK):
+            if scored is not None:
+                peak = score_chunk(*scored, n, peak)
+            if applied is not None:
+                acc = apply_chunk(*applied, n, top, acc)
+        next_top = None if peak is None else jnp.max(peak, axis=1, keepdims=True)
+        return next_top, acc
+
+    def keep(q, top, acc):
+        acc_ref[q] = acc
+        m_ref[q] = jnp.broadcast_to(top, (QH * BLK, HD))
+
+    def finish(q, top2, acc2):
+        top1 = m_ref[q]
+        top = jnp.maximum(top1, top2)
+        f1 = jnp.exp2((top1 - top) * FACTOR)
+        f2 = jnp.exp2((top2 - top) * FACTOR)
+        total = f1 * acc_ref[q, :, HD:] + f2 * acc2[:, HD:]
+        whole = ((f1 * acc_ref[q, :, :HD] + f2 * acc2[:, :HD]) / total).astype(jnp.bfloat16)
+        for h in range(QH):
+            out_ref[q * BLK : (q + 1) * BLK, h * HD : (h + 1) * HD] = whole[h * BLK : (h + 1) * BLK]
+
+    inputs[2].wait()
+    for q in range(2):
+        queries_of.append(
+            jnp.concatenate([qs[q * BLK : (q + 1) * BLK, h * HD : (h + 1) * HD] for h in range(QH)], axis=0)
+        )
+
+    @pl.when(z < 2)
+    def _():
         def load(n, _):
             q = n // PART
             s = n % PART
-            block = list_ref[2 * y + q, part * PART + s]
+            block = list_ref[2 * y + q, s]
             rows = pl.ds(pl.multiple_of(s * BLK, BLK), BLK)
             kc[q, rows, :] = block_of(0, block)
             vc[q, rows, :] = block_of(1, block)
@@ -385,66 +454,7 @@
 
         lax.fori_loop(0, 2 * PART, load, 0)
 
-    def keys_of(q, part, masked, n):
-        if masked:
-            return kc[q, n * CHUNK * BLK : (n + 1) * CHUNK * BLK, :]
-        return vbuf[0, n].reshape(CHUNK * BLK, HD)
-
-    def values_of(q, part, masked, n):
-        if masked:
-            return vc[q, n * CHUNK * BLK : (n + 1) * CHUNK * BLK, :]
-        return vbuf[1, n].reshape(CHUNK * BLK, HD)
-
-    def attend(q, part, masked=True):
-        my_block = 8 * p + 2 * y + q
-        count = count_ref[2 * y + q]
-        rows = pl.ds(pl.multiple_of(q * BLK, BLK), BLK)
-        q4 = jnp.concatenate([qs[rows, h * HD : (h + 1) * HD] for h in range(QH)], axis=0)
-        width = CHUNK * BLK
-        peak = None
-        for n in range(PART // CHUNK):
-            keys = keys_of(q, part, masked, n)
-            scores = lax.dot_general(q4, keys, (((1,), (1,)), ((), ())), preferred_element_type=jnp.float32)
-            for k in range(CHUNK):
-                if not masked:
-                    tile = scores[:, k * BLK : (k + 1) * BLK]
-                    peak = tile if peak is None else jnp.maximum(peak, tile)
-                    continue
-                slot = part * PART + n * CHUNK + k
-                block = list_ref[2 * y + q, slot]
-                reach = jnp.where(block == my_block, 0, BLK)
-                reach = jnp.where(slot < count, reach, -BLK)
-                ok = delta <= reach
-                tile = scores[:, k * BLK : (k + 1) * BLK].reshape(QH, BLK, BLK)
-                tile = jnp.where(ok[None], tile, MASKED).reshape(QH * BLK, BLK)
-                s_ref[:, (n * CHUNK + k) * BLK : (n * CHUNK + k + 1) * BLK] = tile
-                peak = tile if peak is None else jnp.maximum(peak, tile)
-            if not masked:
-                s_ref[:, n * width : (n + 1) * width] = scores
-        top = jnp.max(peak, axis=1, keepdims=True)
-        total = None
-        acc = None
-        for n in range(PART // CHUNK):
-            weights = jnp.exp2((s_ref[:, n * width : (n + 1) * width] - top) * FACTOR)
-            for k in range(CHUNK):
-                tile = weights[:, k * BLK : (k + 1) * BLK]
-                total = tile if total is None else total + tile
-            values = values_of(q, part, masked, n)
-            out = jnp.dot(weights.astype(jnp.bfloat16), values, preferred_element_type=jnp.float32)
-            acc = out if acc is None else acc + out
-        return top, jnp.sum(total, axis=1, keepdims=True), acc
-
-    inputs[2].wait()
-    load_part(1)
-
-    def first(q, _):
-        top, total, acc = attend(q, 1)
-        acc_ref[q] = acc
-        m_ref[q] = jnp.broadcast_to(top, (QH * BLK, HD))
-        l_ref[q] = jnp.broadcast_to(total, (QH * BLK, HD))
-        return 0
-
-    lax.fori_loop(0, 1, first, 0)
+    top_s0, _ = stage((0, 1), None, None)
 
     @pl.when(z >= 2)
     def _():
@@ -456,39 +466,21 @@
                     v2_copy(cc, i).wait_recv()
                 vs_copy(cc).start()
 
-    lax.fori_loop(1, 2, first, 0)
-
-    def second(q, masked):
-        top2, total2, acc2 = attend(q, 0, masked)
-        top1 = m_ref[q]
-        top = jnp.maximum(top1, top2)
-        f1 = jnp.exp2((top1 - top) * FACTOR)
-        f2 = jnp.exp2((top2 - top) * FACTOR)
-        whole = (f1 * acc_ref[q] + f2 * acc2) / (f1 * l_ref[q] + f2 * total2)
-        whole = whole.astype(jnp.bfloat16)
-        rows = pl.ds(pl.multiple_of(q * BLK, BLK), BLK)
-        for h in range(QH):
-            out_ref[rows, h * HD : (h + 1) * HD] = whole[h * BLK : (h + 1) * BLK]
+    top_s1, acc_s0 = stage((1, 1), (0, 1), top_s0)
+    keep(0, top_s0, acc_s0)
 
     @pl.when(z >= 2)
     def _():
         vs_copy(1 - c).wait_recv()
-
-        def gathered(q, _):
-            second(q, False)
-            return 0
-
-        lax.fori_loop(0, 2, gathered, 0)
-
-    @pl.when(z < 2)
-    def _():
-        load_part(0)
-
-        def windowed(q, _):
-            second(q, True)
-            return 0
-
-        lax.fori_loop(0, 2, windowed, 0)
+        kc[0] = vbuf[0].reshape(PART * BLK, HD)
+        vc[0] = vbuf[1].reshape(PART * BLK, HD)
+
+    top_v0, acc_s1 = stage((0, 0), (1, 1), top_s1)
+    keep(1, top_s1, acc_s1)
+    top_v1, acc_v0 = stage((1, 0), (0, 0), top_v0)
+    finish(0, top_v0, acc_v0)
+    _, acc_v1 = stage(None, (1, 0), top_v1)
+    finish(1, top_v1, acc_v1)
 
     for kv in range(2):
 
@@ -574,9 +566,8 @@
             pltpu.VMEM((2 * BLK, QH * HD), jnp.bfloat16),
             pltpu.VMEM((2, PART * BLK, HD), jnp.bfloat16),
             pltpu.VMEM((2, PART * BLK, HD), jnp.bfloat16),
-            pltpu.VMEM((QH * BLK, PART * BLK), jnp.float32),
-            pltpu.VMEM((2, QH * BLK, HD), jnp.float32),
-            pltpu.VMEM((2, QH * BLK, HD), jnp.float32),
+            pltpu.VMEM((2, QH * BLK, PART * BLK), jnp.float32),
+            pltpu.VMEM((2, QH * BLK, 2 * HD), jnp.float32),
             pltpu.VMEM((2, QH * BLK, HD), jnp.float32),
             pltpu.VMEM((2, 4, BLK, HD), jnp.bfloat16),
             pltpu.VMEM((2, 3, BLK, HD), jnp.bfloat16),

time: 72.8 us -> 67.2 us (0.923)
  Pallas kernels: 71 us -> 65.3 us
    pallas_call x1, Pallas kernels: 71 us -> 65.3 us  [local_attention(): pl.pallas_call(attention_kernel, out_shape=jax.ShapeDtypeStruct((rows, QH...]
where the time goes in v4:
time: 67.2 us; the launch traced here: 67 us
  Pallas kernels  65.3 us (97%)
  local copies, waits for them, and re-layouts  1.67 us (2%)
    pallas_call x1, Pallas kernels, local_attention(): pl.pallas_call(attention_kernel, out_shape=jax.ShapeDtypeStruct((rows, QH...  65.3 us
    unnamed x1, local copies, waits for them, and re-layouts  1.67 us

profile of v4, /device:TPU:95, one launch (start us, length us, event | category | flops | bytes accessed | tf_op | source)
XLA Modules:
  0.0 67.0 jit_solution(16160433651191184316)
XLA Ops:
  0.0 65.3 %shard_map.55 = bf16[256,512]{1,0:T(8,128)(2,1)} custom-call(s32[8,32]{1,0:T(8,128)} %list_hbm.1, s32[8]{0:T(128)} %count_hbm.1, bf16[1024,512]{1,0:T(8,128)(2,1)} %q_hbm.1, bf16[2,128,128]{2,1,0:T(8,128)(2,1)} %bitcast.2, bf16[2,128,128]{2,1,0:T(8,128)(2,1)} %bitcast.3), custom_call_target="tpu_custom_call" | custom-call | tf_op jit(solution)/shard_map/pallas_call | solution.py:549
  65.3 1.7 %copy.7 = bf16[256,512]{1,0:T(8,128)(2,1)} copy(bf16[256,512]{1,0:T(8,128)(2,1)} %shard_map.55) | data formatting | bytes 524288

commit v5 on v4

--- a/solution.py
+++ b/solution.py
@@ -21,11 +21,12 @@
 
 def attention_kernel(
     list_hbm, count_hbm, q_hbm, k_hbm, v_hbm, out_ref,
-    list_ref, count_ref, pick_ref,
-    buf, vbuf, qs, kc, vc, s_ref, acc_ref, m_ref, part_out, part_in, half_out, half_in,
+    list_ref, count_ref, pick_ref, told_ref, list_vm,
+    k_win, v_win, vbuf, qs, kc, vc, s_ref, acc_ref, m_ref, part_out, part_in, half_out, half_in,
     in_sem, z_send, z_recv, f_send, p1_send, p1_recv, p2_send, p2_recv, f2_send, f2_recv, sib_send, sib_recv,
-    vp_send, vp_recv, vh_send, vh_recv, vz_send, vz_recv, v1_send, v1_recv, v2_send, v2_recv, vs_send, vs_recv,
+    vp_send, vp_recv, vh_send, vh_recv, vz_send, vz_recv, v1_send, v1_recv, v2_send, v2_recv, vs_send, vs_recv, tell_send, tell_recv,
 ):
+    win = (k_win, v_win)
     p = lax.axis_index("pb")
     y = lax.axis_index("ka")
     z = p // 8
@@ -85,9 +86,9 @@
     partners.append((always, (z, x, 1 - c, y)))
     partners.append((z >= 1, (jnp.maximum(z - 1, 0), x, c, y)))
     partners.append((z <= 6, (jnp.minimum(z + 1, 7), x, c, y)))
-    for i in range(5):
-        partners.append((z == 2, (3 + i, x, c, y)))
-    partners.append((z >= 3, (2, x, c, y)))
+    for i in range(6):
+        partners.append((z == 1, (2 + i, x, c, y)))
+    partners.append((z >= 2, (1, x, c, y)))
     for kv in range(2):
         there = z_target(kv)
         partners.append((jnp.logical_not(here(there)), there))
@@ -106,7 +107,7 @@
     pl.semaphore_wait(barrier, expected)
 
     def z_copy(kv):
-        region = buf.at[kv, z_half, g_own, x, c]
+        region = win[kv].at[z_half, g_own, x, c]
         return remote(src[kv], region, z_send.at[kv], z_recv.at[kv, z_half], dev(*z_target(kv)))
 
     for kv in range(2):
@@ -118,7 +119,7 @@
 
         @pl.when(own)
         def _():
-            pltpu.make_async_copy(src[kv], buf.at[kv, z_half, g_own, x, c], z_recv.at[kv, z_half]).start()
+            pltpu.make_async_copy(src[kv], win[kv].at[z_half, g_own, x, c], z_recv.at[kv, z_half]).start()
 
     def row(kv):
         return y if kv == 0 else x
@@ -135,23 +136,23 @@
     sibling = dev(z, x, 1 - c, y)
 
     def p1_copy(kv, hi, i):
-        region = buf.at[kv, hi, row(kv), col(kv), c]
+        region = win[kv].at[hi, row(kv), col(kv), c]
         return remote(region, region, p1_send.at[kv, hi, i - 1], p1_recv.at[kv, hi, i - 1], along(kv, i))
 
     def p1_live(kv, hi, i):
         if kv == 1:
             return have(hi)
         wanted = needed(hi, y, (x + i) % 4)
-        return wanted | (z == 2) if hi == 0 else wanted
+        return wanted | (z == 1) if hi == 2 else wanted
 
     def p1_got(kv, hi):
         if kv == 1:
             return have(hi)
         wanted = needed(hi, y, x)
-        return wanted | (z == 2) if hi == 0 else wanted
+        return wanted | (z == 1) if hi == 2 else wanted
 
     def p2_copy(kv, hi, i):
-        region = buf.at[kv, hi, row(kv), :, c]
+        region = win[kv].at[hi, row(kv), :, c]
         return remote(region, region, p2_send.at[kv, hi, i - 1], p2_recv.at[kv, hi, i - 1], across(kv, i))
 
     def relayed(kv, hi):
@@ -159,18 +160,18 @@
 
     def far_copy(kv, hi, i):
         g, first = (row(kv) + 4 - i) % 4, 0 if i == 1 else 2
-        region = buf.at[kv, hi, g, first : first + 2, c]
+        region = win[kv].at[hi, g, first : first + 2, c]
         return remote(region, region, f2_send.at[kv, hi, i // 2], f2_recv.at[kv, hi, i // 2], across(kv, i))
 
     def p2_live(kv, hi, i):
         return needed(hi, y, x) if kv == 0 else needed(hi, x, (x + i) % 4)
 
     def sib_copy(kv, hi, g):
-        region = buf.at[kv, hi, g, :, c]
+        region = win[kv].at[hi, g, :, c]
         return remote(region, region, sib_send.at[kv, hi, g], sib_recv.at[kv, hi, g], sibling)
 
     def vz_copy(i):
-        return remote(vbuf.at[c, x, y], vbuf.at[c, x, y], vz_send.at[i], vz_recv, dev(3 + i, x, c, y))
+        return remote(vbuf.at[c, x, y], vbuf.at[c, x, y], vz_send.at[i], vz_recv, dev(2 + i, x, c, y))
 
     def v_line(first, i):
         to_x = (c == 0) == first
@@ -187,8 +188,8 @@
         return remote(vbuf.at[cc], vbuf.at[cc], vs_send, vs_recv, sibling)
 
     def f_copy(kv, up):
-        region = buf.at[kv, 1, row(kv), col(kv), c]
-        there = buf.at[kv, 0 if up else 2, row(kv), col(kv), c]
+        region = win[kv].at[1, row(kv), col(kv), c]
+        there = win[kv].at[0 if up else 2, row(kv), col(kv), c]
         to = jnp.minimum(z + 1, 7) if up else jnp.maximum(z - 1, 0)
         return remote(region, there, f_send.at[kv, int(up)], z_recv.at[kv, 0 if up else 2], dev(to, x, c, y))
 
@@ -198,9 +199,19 @@
     for copy in inputs[:2]:
         copy.wait()
 
+    tell = remote(list_hbm, list_vm, tell_send, tell_recv, dev(1, x, c, y))
+
     @pl.when(z == 2)
     def _():
-        entries = [list_ref[2 * y, i] for i in range(NV)]
+        tell.start()
+
+    @pl.when(z == 1)
+    def _():
+        tell.wait_recv()
+        told = pltpu.make_async_copy(list_vm, told_ref, in_sem.at[3])
+        told.start()
+        told.wait()
+        entries = [told_ref[0, i] for i in range(NV)]
         slots = [4 * x + (y + i) % 4 for i in range(4)] + [4 * ((x + i) % 4) + y for i in range(4)]
         chosen = [jnp.int32(-1)] * 8
         for i in range(NV):
@@ -217,7 +228,7 @@
 
             @pl.when(have(hi))
             def _():
-                pltpu.make_async_copy(src[kv], buf.at[kv, hi, row(kv), col(kv), c], z_recv.at[kv, hi]).wait()
+                pltpu.make_async_copy(src[kv], win[kv].at[hi, row(kv), col(kv), c], z_recv.at[kv, hi]).wait()
 
             if hi == 1:
                 for up in (False, True):
@@ -238,7 +249,7 @@
 
                 @pl.when(p1_got(kv, hi))
                 def _():
-                    region = buf.at[kv, hi, row(kv), (col(kv) + 4 - i) % 4, c]
+                    region = win[kv].at[hi, row(kv), (col(kv) + 4 - i) % 4, c]
                     remote(region, region, p1_send.at[kv, hi, i - 1], p1_recv.at[kv, hi, i - 1], sibling).wait_recv()
 
     def p2_start(hi, when):
@@ -260,14 +271,14 @@
 
                 @pl.when(needed(hi, g, x))
                 def _():
-                    region = buf.at[kv, hi, g, :, c]
+                    region = win[kv].at[hi, g, :, c]
                     remote(region, region, p2_send.at[kv, hi, i - 1], p2_recv.at[kv, hi, i - 1], sibling).wait_recv()
                     if relayed(kv, hi):
                         far_copy(kv, hi, i).start()
                     sib_copy(kv, hi, g).start()
 
-    def far(hi):
-        for kv in range(2):
+    def far(hi, kvs=(0, 1)):
+        for kv in kvs:
             g = (row(kv) + 2) % 4
 
             @pl.when(needed(hi, g, x))
@@ -275,10 +286,10 @@
                 if relayed(kv, hi):
                     for i in (1, 3):
                         first = 0 if i == 1 else 2
-                        region = buf.at[kv, hi, g, first : first + 2, c]
+                        region = win[kv].at[hi, g, first : first + 2, c]
                         remote(region, region, f2_send.at[kv, hi, i // 2], f2_recv.at[kv, hi, i // 2], sibling).wait_recv()
                 else:
-                    region = buf.at[kv, hi, g, :, c]
+                    region = win[kv].at[hi, g, :, c]
                     remote(region, region, p2_send.at[kv, hi, 1], p2_recv.at[kv, hi, 1], sibling).wait_recv()
                 sib_copy(kv, hi, g).start()
 
@@ -291,30 +302,31 @@
         return remote(half_out.at[kv], half_in, vh_send, vh_recv, sibling)
 
     p1_wait(1)
-    p2_start(1, z >= 0)
+    p2_start(1, z != 1)
     p1_wait(0)
-
-    @pl.when(z == 2)
+    p2_start(0, z >= 0)
+    p1_wait(2)
+
+    @pl.when(z == 1)
     def _():
         for kv in range(2):
 
             picked = [jnp.zeros((BLK, HD), jnp.bfloat16)] * 4
-            for hi in range(2):
+            for half_name in range(2):
                 for l in range(4):
                     for r in range(2):
-                        block = buf[kv, hi, row(kv), l, c, r]
-                        name = 64 * hi + 16 * row(kv) + 4 * l + 2 * c + r
+                        block = win[kv][1 + half_name, row(kv), l, c, r]
+                        name = 64 * half_name + 16 * row(kv) + 4 * l + 2 * c + r
                         picked = [jnp.where(pick_ref[4 * kv + i] == name, block, picked[i]) for i in range(4)]
             for i in range(4):
                 part_out[kv, i] = picked[i]
             for i in (1, 3, 2):
                 vp_copy(kv, i).start()
 
-    p2_start(0, z >= 0)
-    p1_wait(2)
+    p2_start(1, z == 1)
     p2_start(2, z >= 0)
 
-    @pl.when(z == 2)
+    @pl.when(z == 1)
     def _():
         for kv in range(2):
             for i in (1, 3, 2):
@@ -323,13 +335,13 @@
         vh_copy(1 - c).start()
         vh_copy(c).wait_recv()
         vbuf[c, x, y] = half_out[c] + half_in[...]
-        for i in (0, 4, 1, 3, 2):
+        for i in (0, 5, 1, 4, 2, 3):
             vz_copy(i).start()
 
     near(1)
     near(0)
 
-    @pl.when(z >= 3)
+    @pl.when(z >= 2)
     def _():
         vz_copy(0).wait_recv()
 
@@ -354,13 +366,13 @@
 
     far(0)
     far(2)
-    for hi in (1, 0, 2):
-        for kv in range(2):
+    def window_wait(kv):
+        for hi in (1, 0, 2):
             for g in range(4):
 
                 @pl.when(needed(hi, g, x))
                 def _():
-                    region = buf.at[kv, hi, g, :, 1 - c]
+                    region = win[kv].at[hi, g, :, 1 - c]
                     remote(region, region, sib_send.at[kv, hi, g], sib_recv.at[kv, hi, g], sibling).wait_recv()
 
     def place(block):
@@ -369,7 +381,7 @@
 
     def block_of(kv, block):
         hi, g, l, cc, r = place(block)
-        return buf[kv, hi, g, l, cc, r]
+        return win[kv][hi, g, l, cc, r]
 
     delta = lax.broadcasted_iota(jnp.int32, (BLK, BLK), 1) - lax.broadcasted_iota(jnp.int32, (BLK, BLK), 0)
 
@@ -441,6 +453,10 @@
             jnp.concatenate([qs[q * BLK : (q + 1) * BLK, h * HD : (h + 1) * HD] for h in range(QH)], axis=0)
         )
 
+    window_wait(0)
+    top_s0, _ = stage((0, 1), None, None)
+    window_wait(1)
+
     @pl.when(z < 2)
     def _():
         def load(n, _):
@@ -454,8 +470,6 @@
 
         lax.fori_loop(0, 2 * PART, load, 0)
 
-    top_s0, _ = stage((0, 1), None, None)
-
     @pl.when(z >= 2)
     def _():
         for cc in range(2):
@@ -523,11 +537,15 @@
 
     @pl.when(z == 2)
     def _():
+        tell.wait_send()
+
+    @pl.when(z == 1)
+    def _():
         for kv in range(2):
             for i in range(1, 4):
                 vp_copy(kv, i).wait_send()
         vh_copy(1 - c).wait_send()
-        for i in range(5):
+        for i in range(6):
             vz_copy(i).wait_send()
 
     @pl.when(z >= 2)
@@ -561,7 +579,10 @@
             pltpu.SMEM((8, LIST), jnp.int32),
             pltpu.SMEM((8,), jnp.int32),
             pltpu.SMEM((8,), jnp.int32),
-            pltpu.VMEM((2, 3, 4, 4, 2, 2, BLK, HD), jnp.bfloat16),
+            pltpu.SMEM((8, LIST), jnp.int32),
+            pltpu.VMEM((8, LIST), jnp.int32),
+            pltpu.VMEM((3, 4, 4, 2, 2, BLK, HD), jnp.bfloat16),
+            pltpu.VMEM((3, 4, 4, 2, 2, BLK, HD), jnp.bfloat16),
             pltpu.VMEM((2, 4, 4, BLK, HD), jnp.bfloat16),
             pltpu.VMEM((2 * BLK, QH * HD), jnp.bfloat16),
             pltpu.VMEM((2, PART * BLK, HD), jnp.bfloat16),
@@ -573,7 +594,7 @@
             pltpu.VMEM((2, 3, BLK, HD), jnp.bfloat16),
             pltpu.VMEM((2, BLK, HD), jnp.bfloat16),
             pltpu.VMEM((BLK, HD), jnp.bfloat16),
-            dma((3,)),
+            dma((4,)),
             dma((2,)), dma((2, 3)), dma((2, 2)),
             dma((2, 3, 3)), dma((2, 3, 3)),
             dma((2, 3, 3)), dma((2, 3, 3)),
@@ -581,9 +602,10 @@
             dma((2, 3, 4)), dma((2, 3, 4)),
             dma((2, 3)), dma((2, 3)),
             dma, dma,
-            dma((5,)), dma,
+            dma((6,)), dma,
             dma((3,)), dma((3,)),
             dma((3,)), dma((3,)),
+            dma, dma,
             dma, dma,
         ],
         compiler_params=pltpu.CompilerParams(collective_id=0, has_side_effects=True, vmem_limit_bytes=60 * 1024 * 1024),

time: 67.2 us -> 66 us (0.982)
  Pallas kernels: 65.3 us -> 63.7 us
    pallas_call x1, Pallas kernels: 65.3 us -> 63.7 us  [local_attention(): pl.pallas_call(attention_kernel, out_shape=jax.ShapeDtypeStruct((rows, QH...]
where the time goes in v5:
time: 66 us; the launch traced here: 65.3 us
  Pallas kernels  63.7 us (97%)
  local copies, waits for them, and re-layouts  1.67 us (3%)
    pallas_call x1, Pallas kernels, local_attention(): pl.pallas_call(attention_kernel, out_shape=jax.ShapeDtypeStruct((rows, QH...  63.7 us
    unnamed x1, local copies, waits for them, and re-layouts  1.67 us

profile of v5, /device:TPU:95, one launch (start us, length us, event | category | flops | bytes accessed | tf_op | source)
XLA Modules:
  0.0 65.3 jit_solution(14604542292035473357)
XLA Ops:
  0.0 63.7 %shard_map.55 = bf16[256,512]{1,0:T(8,128)(2,1)} custom-call(s32[8,32]{1,0:T(8,128)} %list_hbm.1, s32[8]{0:T(128)} %count_hbm.1, bf16[1024,512]{1,0:T(8,128)(2,1)} %q_hbm.1, bf16[2,128,128]{2,1,0:T(8,128)(2,1)} %bitcast.2, bf16[2,128,128]{2,1,0:T(8,128)(2,1)} %bitcast.3), custom_call_target="tpu_custom_call" | custom-call | tf_op jit(solution)/shard_map/pallas_call | solution.py:567
  63.7 1.7 %copy.7 = bf16[256,512]{1,0:T(8,128)(2,1)} copy(bf16[256,512]{1,0:T(8,128)(2,1)} %shard_map.55) | data formatting | bytes 524288

commit v6 on v5

--- a/solution.py
+++ b/solution.py
@@ -302,7 +302,7 @@
         return remote(half_out.at[kv], half_in, vh_send, vh_recv, sibling)
 
     p1_wait(1)
-    p2_start(1, z != 1)
+    p2_start(1, z >= 0)
     p1_wait(0)
     p2_start(0, z >= 0)
     p1_wait(2)
@@ -323,7 +323,6 @@
             for i in (1, 3, 2):
                 vp_copy(kv, i).start()
 
-    p2_start(1, z == 1)
     p2_start(2, z >= 0)
 
     @pl.when(z == 1)

time: 66 us -> 66 us (level)
  no operation moved by 1% of the time
where the time goes in v6:
time: 66 us; the launch traced here: 65.3 us
  Pallas kernels  63.7 us (97%)
  local copies, waits for them, and re-layouts  1.67 us (3%)
    pallas_call x1, Pallas kernels, local_attention(): pl.pallas_call(attention_kernel, out_shape=jax.ShapeDtypeStruct((rows, QH...  63.7 us
    unnamed x1, local copies, waits for them, and re-layouts  1.67 us

profile of v6, /device:TPU:95, one launch (start us, length us, event | category | flops | bytes accessed | tf_op | source)
XLA Modules:
  0.0 65.3 jit_solution(15046099780760497021)
XLA Ops:
  0.0 63.7 %shard_map.55 = bf16[256,512]{1,0:T(8,128)(2,1)} custom-call(s32[8,32]{1,0:T(8,128)} %list_hbm.1, s32[8]{0:T(128)} %count_hbm.1, bf16[1024,512]{1,0:T(8,128)(2,1)} %q_hbm.1, bf16[2,128,128]{2,1,0:T(8,128)(2,1)} %bitcast.2, bf16[2,128,128]{2,1,0:T(8,128)(2,1)} %bitcast.3), custom_call_target="tpu_custom_call" | custom-call | tf_op jit(solution)/shard_map/pallas_call | solution.py:566
  63.7 1.7 %copy.7 = bf16[256,512]{1,0:T(8,128)(2,1)} copy(bf16[256,512]{1,0:T(8,128)(2,1)} %shard_map.55) | data formatting | bytes 524288
